TPU v7x, 128 devices: a whole 4x4x4 slice. The times are simulated.
128 devices in a mesh: comp: 2 (over y_lo), gx: 8 (over x, y_hi), gy: 8 (over z, core).
Axes of the slice: x: 4, y: 4 (y_hi: 2, y_lo: 2; y = y_hi * 2 + y_lo), z: 4, core: 2. Of those that a mesh axis runs over, the one named last changes fastest.
Arguments:
- state: float32 [2, 30, 256, 2048], P('comp', None, 'gx', 'gy'), may hold values from -6 to 6
- conduct: float32 [2, 30, 256, 2048], P('comp', None, 'gx', 'gy'), may hold values from 0.3 to 3
- storage: float32 [2], P('comp'), may hold values from 0.05 to 0.5
- surface_source: float32 [2, 256, 2048], P('comp', 'gx', 'gy'), may hold values from -6 to 6
- plant_type: int32 [2, 256, 2048], P('comp', 'gx', 'gy'), may hold values from 0 to 15
- plant_table: float32 [16, 2], replicated, may hold values from 0.3 to 3
- layer_weights: float32 [2, 16, 6], replicated, may hold values from 0.05 to 1
- remap_rows: int32 [2, 256], P('comp', 'gx'), may hold values from 0 to 31
- remap_weights: float32 [2, 2048, 128], P('comp', 'gy'), may hold values from 0 to 1
Outputs:
- new_state: float32 [2, 30, 256, 2048], P('comp', None, 'gx', 'gy')
- exchange_flux: float32 [2, 256, 2048], P('comp', 'gx', 'gy')
All inputs are finite; a program needn't handle non-finite values.
Results may differ from a plain program's by a relative error of at most 0.0003.
Values sent between devices are 32-bit elements; how exact they have to be, the bound alone decides.
A program may use at most 64 MiB of HBM per device.

v0:
```python
import jax
import jax.numpy as jnp
from jax import lax
from jax.sharding import PartitionSpec as P

NS = 6
PATCH = 128
PLANTS = 16
ITERS = 3


def from_partner(value, axis, distance):
    mask = 2**distance
    pairs = [(source, source ^ mask) for source in range(lax.axis_size(axis))]
    return lax.ppermute(value, axis, pairs)


def extended(block, sides, width):
    for axis, dim in sides:
        count = lax.axis_size(axis)
        forward = [(i, i + 1) for i in range(count - 1)]
        backward = [(target, source) for source, target in forward]
        low = lax.ppermute(
            lax.slice_in_dim(block, block.shape[dim] - width, None, axis=dim), axis, forward
        )
        high = lax.ppermute(lax.slice_in_dim(block, 0, width, axis=dim), axis, backward)
        block = jnp.concatenate([low, block, high], axis=dim)
    return block


def apply_padded(vp, kp):
    v = vp[1:-1, 1:-1, 1:-1]
    kc = kp[1:-1, 1:-1, 1:-1]
    total = jnp.zeros_like(v)
    moves = [(2, 1, 1), (0, 1, 1), (1, 2, 1), (1, 0, 1), (1, 1, 2), (1, 1, 0)]
    for a, b, e in moves:
        vn = vp[a : a + v.shape[0], b : b + v.shape[1], e : e + v.shape[2]]
        kn = kp[a : a + v.shape[0], b : b + v.shape[1], e : e + v.shape[2]]
        total = total + 0.5 * (kc + kn) * (v - vn)
    return total


def pad_levels(field):
    return jnp.pad(field, ((1, 1), (0, 0), (0, 0)))


def least_squares(hmat, beta):
    gram = jnp.sum(hmat[:, :, None] * hmat[:, None, :], axis=0)
    target_vector = beta * hmat[0, :]
    factor = jnp.linalg.cholesky(gram)
    return jax.scipy.linalg.cho_solve((factor, True), target_vector)


def one_hot_types(kinds):
    return (kinds[None, :, :] == jnp.arange(PLANTS)[:, None, None]).astype(jnp.float32)


def forcing_for(layers, rows, weights, kinds, profile):
    hp = lax.Precision.HIGHEST
    picked = jnp.take(layers, rows, axis=1)
    width = layers.shape[2]
    blocks = picked.reshape(layers.shape[0], layers.shape[1], width // PATCH, PATCH)
    wblk = weights.reshape(width // PATCH, PATCH, PATCH)
    remapped = jnp.einsum("lxbk,bjk->lxbj", blocks, wblk, precision=hp).reshape(layers.shape)
    prof = jnp.einsum("pl,pxy->lxy", profile, one_hot_types(kinds), precision=hp)
    return jnp.sum(prof * remapped, axis=0)


def inner(a, b):
    return lax.psum(jnp.sum(a * b), ("gx", "gy"))


def body(
    state,
    conduct,
    storage,
    surface_source,
    plant_type,
    plant_table,
    layer_weights,
    remap_rows,
    remap_weights,
):
    hp = lax.Precision.HIGHEST
    comp_index = lax.axis_index("comp")
    field = state[0]
    levels = field.shape[0]
    keff = conduct[0] * (1.0 + 0.5 * jnp.tanh(field))
    kinds = plant_type[0]
    own_table = jnp.where(comp_index == 0, layer_weights[0], layer_weights[1])
    other_table = jnp.where(comp_index == 0, layer_weights[1], layer_weights[0])
    layers = field[:NS]
    partner_layers = from_partner(layers, "comp", 0)
    other_force = forcing_for(partner_layers, remap_rows[0], remap_weights[0], kinds, other_table)
    selector = one_hot_types(kinds)
    own_prof = jnp.einsum("pl,pxy->lxy", own_table, selector, precision=hp)
    own_force = jnp.sum(own_prof * layers, axis=0)
    atmospheric_forcing = jnp.where(comp_index == 0, own_force, other_force)
    soil_force = jnp.where(comp_index == 0, other_force, own_force)
    params = jnp.einsum("pq,pxy->qxy", plant_table, selector, precision=hp)
    flux = params[0] * (params[1] * soil_force - atmospheric_forcing)
    sign = 1.0 - 2.0 * comp_index.astype(jnp.float32)
    top = sign * flux[None] * own_prof
    source = jnp.concatenate([top, jnp.zeros((levels - NS,) + flux.shape, jnp.float32)], axis=0)
    source = source.at[0].add(surface_source[0])
    diagonal_shift = storage[0]
    depth = 1
    stacked = jnp.stack([field, keff])
    padded = extended(stacked, (("gx", 2), ("gy", 3)), depth)
    kext = padded[1]

    def apply_extended_operator(vector):
        return apply_padded(pad_levels(vector), pad_levels(kext))

    rhs_rim = 0
    rhs = source - apply_extended_operator(padded[0])
    beta = jnp.sqrt(lax.psum(jnp.sum(rhs * rhs), ("gx", "gy")))
    basis = [rhs / beta]
    rims = [rhs_rim]
    hmat = jnp.zeros((ITERS + 1, ITERS), jnp.float32)
    for j in range(ITERS):
        operate_vector = basis[j]
        padded_vector = extended(operate_vector, (("gx", 1), ("gy", 2)), 1)
        krylov_vector = diagonal_shift * operate_vector + apply_extended_operator(padded_vector)
        near = [basis[i] for i in range(j + 1)]
        for i in range(j + 1):
            h = inner(krylov_vector, near[i])
            krylov_vector = krylov_vector - h * near[i]
            hmat = hmat.at[i, j].set(h)
        nrm = jnp.sqrt(inner(krylov_vector, krylov_vector))
        hmat = hmat.at[j + 1, j].set(nrm)
        if j + 1 < ITERS:
            basis.append(krylov_vector / nrm)
            rims.append(0)
    coef = least_squares(hmat, beta)
    update = field
    for j in range(ITERS):
        update = update + coef[j] * basis[j]
    return (update[None], flux[None])


def solution(mesh):
    in_specs = (
        P("comp", None, "gx", "gy"),
        P("comp", None, "gx", "gy"),
        P("comp"),
        P("comp", "gx", "gy"),
        P("comp", "gx", "gy"),
        P(),
        P(),
        P("comp", "gx"),
        P("comp", "gy", None),
    )
    out_specs = (P("comp", None, "gx", "gy"), P("comp", "gx", "gy"))
    return jax.shard_map(body, mesh=mesh, in_specs=in_specs, out_specs=out_specs, check_vma=False)
```

profile of v0, /device:TPU:1, one launch (start us, length us, event | category | flops | bytes accessed | tf_op | source)
XLA Modules:
  0.0 1806.3 jit_solution(13747439018834869496)
XLA Ops:
  2.5 2.2 collective-permute-start
  4.7 1.7 add_multiply_fusion
  6.5 4.5 collective-permute-start.1
  15.5 2.0 collective-permute-done.2
  17.9 1.4 fusion.110
  19.3 1.8 copy.131
  21.1 5.8 collective-permute-start.3
  28.0 1.9 collective-permute-start.4
  33.5 2.3 copy.134
  35.9 3.2 pad_maximum_fusion
  39.1 1.5 slice_bitcast_fusion.1
  40.6 1.7 gather_fusion
  44.8 5.6 multiply_reduce_fusion.9
  50.4 161.0 %psum.70 = f32[]{:T(128)} all-reduce(f32[]{:T(128)} %get-tuple-element.142), channel_id=1, replica_groups=mesh['comp'=2,'gx'=8,'gy'=8] {'gx','gy'}, use_global_device_ids=true, to_apply=%region_3.4 | all-reduce | flops 1 | bytes 8 | tf_op jit(solution)/shard_map/psum | solution.py:117
  214.9 4.8 collective-permute-done.6
  220.4 3.7 collective-permute-start.7
  224.4 7.8 collective-permute-start.8
  235.2 2.4 select_maximum_fusion.8
  237.7 5.0 multiply_reduce_fusion.8
  242.6 161.8 %psum.71 = f32[]{:T(128)} all-reduce(f32[]{:T(128)} %get-tuple-element.140), channel_id=1, replica_groups=mesh['comp'=2,'gx'=8,'gy'=8] {'gx','gy'}, use_global_device_ids=true, to_apply=%region_5.6 | all-reduce | flops 1 | bytes 8 | tf_op jit(solution)/shard_map/psum | solution.py:70
  404.4 2.6 multiply_reduce_fusion.7
  407.1 164.2 %psum.72 = f32[]{:T(128)} all-reduce(f32[]{:T(128)} %multiply_reduce_fusion.7), channel_id=1, replica_groups=mesh['comp'=2,'gx'=8,'gy'=8] {'gx','gy'}, use_global_device_ids=true, to_apply=%region_7.8 | all-reduce | flops 1 | bytes 8 | tf_op jit(solution)/shard_map/psum | solution.py:70
  572.0 1.9 broadcast_divide_fusion.1
  575.3 5.5 collective-permute-start.9
  584.5 1.9 collective-permute-start.11
  587.8 3.1 collective-permute-start.12
  594.0 2.4 select_maximum_fusion.4
  596.5 4.9 multiply_reduce_fusion.6
  601.3 161.8 %psum.73 = f32[]{:T(128)} all-reduce(f32[]{:T(128)} %get-tuple-element.138), channel_id=1, replica_groups=mesh['comp'=2,'gx'=8,'gy'=8] {'gx','gy'}, use_global_device_ids=true, to_apply=%region_9.10 | all-reduce | flops 1 | bytes 8 | tf_op jit(solution)/shard_map/psum | solution.py:70
  763.1 2.6 multiply_reduce_fusion.5
  766.3 164.4 %psum.74 = f32[]{:T(128)} all-reduce(f32[]{:T(128)} %multiply_reduce_fusion.5), channel_id=1, replica_groups=mesh['comp'=2,'gx'=8,'gy'=8] {'gx','gy'}, use_global_device_ids=true, to_apply=%region_11.12 | all-reduce | flops 1 | bytes 8 | tf_op jit(solution)/shard_map/psum | solution.py:70
  930.7 3.2 multiply_reduce_fusion.4
  933.9 163.2 %psum.75 = f32[]{:T(128)} all-reduce(f32[]{:T(128)} %get-tuple-element.136), channel_id=1, replica_groups=mesh['comp'=2,'gx'=8,'gy'=8] {'gx','gy'}, use_global_device_ids=true, to_apply=%region_13.14 | all-reduce | flops 1 | bytes 8 | tf_op jit(solution)/shard_map/psum | solution.py:70
  1100.6 4.8 collective-permute-done.14
  1108.2 1.9 collective-permute-start.15
  1111.5 3.0 collective-permute-start.16
  1116.3 1.9 scatter.34
  1121.3 2.7 select_maximum_fusion
  1124.0 5.2 multiply_reduce_fusion.3
  1129.2 161.8 %psum.76 = f32[]{:T(128)} all-reduce(f32[]{:T(128)} %get-tuple-element.134), channel_id=1, replica_groups=mesh['comp'=2,'gx'=8,'gy'=8] {'gx','gy'}, use_global_device_ids=true, to_apply=%region_16.17 | all-reduce | flops 1 | bytes 8 | tf_op jit(solution)/shard_map/psum | solution.py:70
  1291.0 2.7 multiply_reduce_fusion.2
  1293.8 164.3 %psum.77 = f32[]{:T(128)} all-reduce(f32[]{:T(128)} %multiply_reduce_fusion.2), channel_id=1, replica_groups=mesh['comp'=2,'gx'=8,'gy'=8] {'gx','gy'}, use_global_device_ids=true, to_apply=%region_18.19 | all-reduce | flops 1 | bytes 8 | tf_op jit(solution)/shard_map/psum | solution.py:70
  1458.2 4.3 multiply_reduce_fusion.1
  1462.5 163.2 %psum.78 = f32[]{:T(128)} all-reduce(f32[]{:T(128)} %get-tuple-element.132), channel_id=1, replica_groups=mesh['comp'=2,'gx'=8,'gy'=8] {'gx','gy'}, use_global_device_ids=true, to_apply=%region_20.21 | all-reduce | flops 1 | bytes 8 | tf_op jit(solution)/shard_map/psum | solution.py:70
  1625.6 3.0 multiply_reduce_fusion
  1628.6 1.8 dynamic-slice.68
  1630.4 163.0 %psum.79 = f32[]{:T(128)} all-reduce(f32[]{:T(128)} %multiply_reduce_fusion), channel_id=1, replica_groups=mesh['comp'=2,'gx'=8,'gy'=8] {'gx','gy'}, use_global_device_ids=true, to_apply=%region_22.23 | all-reduce | flops 1 | bytes 8 | tf_op jit(solution)/shard_map/psum | solution.py:70
  1801.9 4.4 fusion.74
  (147 shorter events, 47.9 us)
Async XLA Ops:
  0.6 41.9 %copy-start = (f32[1,256,128]{2,1,0:T(8,128)S(1)}, f32[1,256,128]{2,1,0:T(8,128)}, u32[]{:S(2)}) copy-start(f32[1,256,128]{2,1,0:T(8,128)} %param.37) | copy-start | bytes 393220
  0.6 5.8 copy-start.2
  2.5 9.8 copy-start.22
  2.5 9.8 copy-start.25
  2.5 10.5 copy-start.19
  2.5 10.5 copy-start.24
  2.5 38.0 %collective-permute-start = (f32[6,32,256]{2,0,1:T(8,128)}, f32[6,32,256]{2,0,1:T(8,128)}, u32[]{:S(2)}, u32[]{:S(2)}) collective-permute-start(f32[6,32,256]{2,0,1:T(8,128)} %bitcast.98), channel_id=1, source_target_pairs={{0,64},{64,0},{1,65},{65,1},{2,66},{66,2},{3,67},{67,3},{4,68},{68... | collective-permute-start | bytes 589832 | tf_op jit(solution)/shard_map/ppermute | solution.py:15
  6.5 9.0 collective-permute-start.1
  11.0 6.5 collective-permute-start.2
  21.1 10.1 collective-permute-start.3
  28.0 5.5 collective-permute-start.4
  39.0 3.3 copy-start.23
  40.6 3.1 copy-start.20
  40.6 3.2 copy-start.18
  42.6 1.4 copy-start.21
  43.3 1.5 copy-start.1
  212.3 2.6 collective-permute-start.5
  213.6 6.1 collective-permute-start.6
  220.4 12.5 collective-permute-start.7
  224.4 9.6 collective-permute-start.8
  235.2 2.4 copy-start.7
  235.2 2.4 copy-start.9
  235.2 2.4 copy-start.12
  235.2 2.5 copy-start.15
  574.0 6.8 collective-permute-start.10
  575.3 6.5 collective-permute-start.9
  581.9 9.0 copy-start.26
  584.5 7.1 collective-permute-start.11
  587.8 5.0 collective-permute-start.12
  594.0 2.4 copy-start.10
  594.0 2.4 copy-start.13
  594.0 2.4 copy-start.16
  594.0 2.5 copy-start.17
  933.9 524.3 %copy-start.4 = (f32[30,32,256]{2,1,0:T(8,128)}, f32[30,32,256]{2,1,0:T(8,128)S(1)}, u32[]{:S(2)}) copy-start(f32[30,32,256]{2,1,0:T(8,128)S(1)} %get-tuple-element.137) | copy-start | bytes 2949124
  1097.9 8.9 copy-start.5
  1098.0 2.6 collective-permute-start.13
  1099.3 6.1 collective-permute-start.14
  1108.2 10.7 collective-permute-start.15
  1111.5 8.6 collective-permute-start.16
  1121.3 2.7 copy-start.6
  1121.3 2.7 copy-start.8
  1121.3 2.7 copy-start.11
  1121.3 2.7 copy-start.14
  1462.5 339.4 %copy-start.3 = (f32[1,30,32,256]{3,2,1,0:T(8,128)S(1)}, f32[1,30,32,256]{3,2,1,0:T(8,128)}, u32[]{:S(2)}) copy-start(f32[1,30,32,256]{3,2,1,0:T(8,128)} %param.29) | copy-start | bytes 2949124
where the time goes:
time: 1810 us
  blocking collectives  1630 us (90%)
  other arithmetic  64.2 us (4%)
  starting transfers between devices  49.1 us (3%)
  local copies, waits for them, and re-layouts  41 us (2%)
    psum x9, blocking collectives, inner(): return lax.psum(jnp.sum(a * b), ('gx', 'gy'))  1470 us
    psum x1, blocking collectives, body(): beta = jnp.sqrt(lax.psum(jnp.sum(rhs * rhs), ('gx', 'gy')))  161 us
  transfers between devices with their start and end apart: 17, of which 6 were waited for; matrix products, arithmetic and copies ran while one was open for 2% of the time, Pallas kernels for 0%

commit v1 on v0

v1 whole, which is shorter than its diff:
```python
import jax
import jax.numpy as jnp
from jax import lax
from jax.experimental import pallas as pl
from jax.experimental.pallas import tpu as pltpu
from jax.sharding import PartitionSpec as P

MESH = pl.DeviceIdType.MESH
F32 = jnp.float32
NS = 6
PATCH = 128
PLANTS = 16
LV = 30
RX = 32
CY = 256
EX = 40
EY = 384
RIM = 3
EDGE = 96
SHIFT = 7.0
HP = lax.Precision.HIGHEST


def roll(x, shift, axis):
    return pltpu.roll(x, shift % x.shape[axis], axis)


def fold(x):
    total = None
    for r in range(0, RX, 8):
        for c in range(0, CY, 128):
            part = x[r : r + 8, c : c + 128]
            total = part if total is None else total + part
    return total


def far_first():
    offsets = []
    for dx in range(4):
        for dh in range(2):
            for dz in range(4):
                for co in range(2):
                    if (dx, dh, dz, co) != (0, 0, 0, 0):
                        hops = min(dx, 4 - dx) + 2 * dh + min(dz, 4 - dz)
                        offsets.append((hops, co, dx, dh, dz))
    return [(dx, dh, dz, co) for _, co, dx, dh, dz in sorted(offsets, reverse=True)]


def kernel(
    state,
    conduct,
    storage,
    surface,
    kinds_in,
    ptab,
    lw,
    rows,
    rw_in,
    out,
    flux_out,
    S,
    K,
    KX,
    KY,
    KZ,
    Q0,
    Q1,
    Q2,
    W0,
    W1,
    PART,
    SURF,
    KINDS,
    RW,
    TAB,
    OWN,
    MASK,
    PL1,
    PH1,
    RL1,
    RH1,
    PL2,
    PH2,
    RL2,
    RH2,
    ROW,
    GATH,
    lsem,
    ssem,
    rsem,
):
    c, gx, gy = lax.axis_index("comp"), lax.axis_index("gx"), lax.axis_index("gy")
    xp, xm = lax.rem(gx + 1, 8), lax.rem(gx + 7, 8)
    yp, ym = lax.rem(gy + 1, 8), lax.rem(gy + 7, 8)
    partner = (1 - c, gx, gy)

    local = [
        pltpu.make_async_copy(state.at[0], S.at[pl.ds(1, LV), pl.ds(0, RX), pl.ds(0, CY)], lsem.at[0]),
        pltpu.make_async_copy(conduct.at[0], K.at[pl.ds(1, LV), pl.ds(0, RX), pl.ds(0, CY)], lsem.at[1]),
        pltpu.make_async_copy(surface.at[0], SURF, lsem.at[2]),
        pltpu.make_async_copy(kinds_in.at[0], KINDS, lsem.at[3]),
        pltpu.make_async_copy(rw_in.at[0], RW, lsem.at[4]),
    ]
    for copy in local:
        copy.start()

    peers = [
        (
            c,
            lax.rem(gx // 2 + dx, 4) * 2 + lax.rem(gx + dh, 2),
            lax.rem(gy // 2 + dz, 4) * 2 + lax.rem(gy + co, 2),
        )
        for dx, dh, dz, co in far_first()
    ]
    barrier = pltpu.get_barrier_semaphore()
    for peer in peers + [partner]:
        pl.semaphore_signal(barrier, inc=1, device_id=peer, device_id_type=MESH)

    zero = jnp.zeros((EX, EY), F32)
    for ref in (S, K, Q0, Q1, Q2):
        ref[0] = zero
        ref[LV + 1] = zero
    row = lax.broadcasted_iota(jnp.int32, (EX, EY), 0)
    col = lax.broadcasted_iota(jnp.int32, (EX, EY), 1)
    row_ok = (
        (row < RX)
        | ((row < RX + RIM) & (gx < 7))
        | ((row >= EX - RIM) & (gx > 0))
    )
    col_ok = (
        (col < CY)
        | ((col < CY + RIM) & (gy < 7))
        | ((col >= EY - RIM) & (gy > 0))
    )
    MASK[...] = jnp.where(row_ok & col_ok, 1.0, 0.0).astype(F32)

    local[0].wait()
    local[1].wait()
    lane = lax.broadcasted_iota(jnp.int32, (RX, 128), 1)

    def edges(value, l, low, high):
        own = (lane >= RIM * l) & (lane < RIM * l + RIM)
        low = jnp.where(own, pltpu.roll(value[:, 0:128], RIM * l, 1), low)
        high = jnp.where(own, pltpu.roll(value[:, 128:256], RIM * l + RIM, 1), high)
        return low, high

    def make_keff(l, carry):
        low, high = carry
        s = S[l + 1, 0:RX, 0:CY]
        k = K[l + 1, 0:RX, 0:CY] * (1.0 + 0.5 * jnp.tanh(s))
        K[l + 1, 0:RX, 0:CY] = k
        low, high = edges(k, l, low, high)
        own = lane == EDGE + l
        low = jnp.where(own, pltpu.roll(s[:, 0:128], EDGE + l, 1), low)
        high = jnp.where(own, pltpu.roll(s[:, 128:256], EDGE + 1 + l, 1), high)
        return low, high

    blank = jnp.zeros((RX, 128), F32)
    low, high = lax.fori_loop(0, LV, make_keff, (blank, blank))
    PL1[...] = low
    PH1[...] = high

    pl.semaphore_wait(barrier, len(peers) + 1)

    sends = []

    def send(src, dst, device):
        i = len(sends)
        copy = pltpu.make_async_remote_copy(
            src_ref=src,
            dst_ref=dst,
            send_sem=ssem.at[i],
            recv_sem=rsem.at[i],
            device_id=device,
            device_id_type=MESH,
        )
        copy.start()
        sends.append(copy)
        return copy

    own_levels, own_columns = pl.ds(1, LV), pl.ds(0, CY)

    def send_rows(ref, width):
        return [
            send(
                ref.at[own_levels, pl.ds(0, width), own_columns],
                ref.at[own_levels, pl.ds(RX, width), own_columns],
                (c, xm, gy),
            ),
            send(
                ref.at[own_levels, pl.ds(RX - width, width), own_columns],
                ref.at[own_levels, pl.ds(EX - width, width), own_columns],
                (c, xp, gy),
            ),
        ]

    def send_packs(low_pack, high_pack, from_low, from_high):
        made = [
            send(low_pack, from_high.at[pl.ds(0, RX)], (c, gx, ym)),
            send(high_pack, from_low.at[pl.ds(0, RX)], (c, gx, yp)),
        ]
        for pack, landing, y in ((low_pack, from_high, ym), (high_pack, from_low, yp)):
            made.append(send(pack.at[pl.ds(0, RIM)], landing.at[pl.ds(RX, RIM)], (c, xm, y)))
            made.append(
                send(pack.at[pl.ds(RX - RIM, RIM)], landing.at[pl.ds(EX - RIM, RIM)], (c, xp, y))
            )
        return made

    levels_copy = send(state.at[0, pl.ds(0, NS)], PART, partner)
    first = send_rows(S, 1) + send_rows(K, RIM) + send_packs(PL1, PH1, RL1, RH1)

    local[2].wait()
    local[3].wait()
    local[4].wait()

    def look_up(r, carry):
        at = pl.ds(pl.multiple_of(r * 8, 8), 8)
        kinds = KINDS[at, :]
        found = [jnp.zeros((8, CY), F32) for _ in range(2 + 2 * NS)]
        for p in range(PLANTS):
            hit = kinds == p
            values = [ptab[p, 0], ptab[p, 1]]
            values += [lw[c, p, l] for l in range(NS)] + [lw[1 - c, p, l] for l in range(NS)]
            found = [jnp.where(hit, v, f) for v, f in zip(values, found)]
        for t, f in enumerate(found):
            TAB[t, at, :] = f
        own = jnp.zeros((8, CY), F32)
        for l in range(NS):
            own = own + found[2 + l] * S[l + 1, at, 0:CY]
        OWN[at, :] = own
        return carry

    lax.fori_loop(0, RX // 8, look_up, 0)
    pick_row = lax.broadcasted_iota(jnp.int32, (RX, RX), 0)
    pick_col = lax.broadcasted_iota(jnp.int32, (RX, RX), 1)
    wanted = jnp.zeros((RX, RX), jnp.int32)
    for x in range(RX):
        wanted = jnp.where(pick_row == x, rows[0, x], wanted)
    picker = jnp.where(wanted == pick_col, 1.0, 0.0).astype(F32)

    for copy in first:
        copy.wait_recv()

    mask = MASK[...]
    rim_lane = lax.broadcasted_iota(jnp.int32, (EX, 128), 1)

    def rim_tile(low_pack, high_pack, l):
        right = pltpu.roll(high_pack, lax.rem(128 - RIM * l, 128), 1)
        left = pltpu.roll(low_pack, lax.rem(253 - RIM * l, 128), 1)
        return jnp.where(rim_lane < RIM, right, jnp.where(rim_lane >= 128 - RIM, left, 0.0))

    def store_rim(ref, l, tile):
        ref[l, :, CY:EY] = jnp.where(mask[:, CY:EY] > 0.0, tile, 0.0)
        ref[l, RX:EX, 0:CY] = jnp.where(mask[RX:EX, 0:CY] > 0.0, ref[l, RX:EX, 0:CY], 0.0)

    def pairs(l, below):
        at = l - 1
        low_pack, high_pack = RL1[...], RH1[...]
        tile = rim_tile(low_pack, high_pack, at)
        k = jnp.concatenate([K[l, :, 0:CY], tile], axis=1)
        k = jnp.where(mask > 0.0, k, 0.0)
        KX[l] = 0.5 * (k + roll(k, -1, 0))
        KY[l] = 0.5 * (k + roll(k, -1, 1))
        KZ[l - 1] = 0.5 * (below + k)
        right = pltpu.roll(high_pack, 32 - at, 1)
        left = pltpu.roll(low_pack, 31 - at, 1)
        s_tile = jnp.where(rim_lane < 1, right, jnp.where(rim_lane >= 127, left, 0.0))
        store_rim(S, l, s_tile)
        return k

    top = lax.fori_loop(1, LV + 1, pairs, zero)
    KZ[LV] = 0.5 * top

    def flow(ref, l, v, down):
        fx = KX[l] * (v - roll(v, -1, 0))
        fy = KY[l] * (v - roll(v, -1, 1))
        up = KZ[l] * (v - ref[l + 1])
        return (fx - roll(fx, 1, 0)) + (fy - roll(fy, 1, 1)) + (up - down), up

    def residual(l, down):
        total, up = flow(S, l, S[l], down)
        Q0[l, 0:RX, 0:CY] = -total[0:RX, 0:CY]
        return up

    lax.fori_loop(1, LV + 1, residual, KZ[0] * (zero - S[1]))

    levels_copy.wait_recv()
    received = PART[...].reshape(NS * RX, CY)
    mixed = jnp.concatenate(
        [
            lax.dot_general(
                received[:, b : b + PATCH],
                RW[b : b + PATCH, :],
                (((1,), (1,)), ((), ())),
                precision=HP,
                preferred_element_type=F32,
            )
            for b in range(0, CY, PATCH)
        ],
        axis=1,
    )
    other = jnp.zeros((RX, CY), F32)
    for l in range(NS):
        remapped = jnp.dot(
            picker, mixed[l * RX : (l + 1) * RX], precision=HP, preferred_element_type=F32
        )
        other = other + TAB[2 + NS + l] * remapped
    own = OWN[...]
    is_air = c == 0
    air = jnp.where(is_air, own, other)
    soil = jnp.where(is_air, other, own)
    flux = TAB[0] * (TAB[1] * soil - air)
    flux_out[0] = flux
    signed = jnp.where(is_air, flux, -flux)
    for l in range(NS):
        value = Q0[l + 1, 0:RX, 0:CY] + signed * TAB[2 + l]
        if l == 0:
            value = value + SURF[...]
        Q0[l + 1, 0:RX, 0:CY] = value

    def pack_rhs(l, carry):
        return edges(Q0[l + 1, 0:RX, 0:CY], l, *carry)

    low, high = lax.fori_loop(0, LV, pack_rhs, (blank, blank))
    PL2[...] = low
    PH2[...] = high
    second = send_rows(Q0, RIM) + send_packs(PL2, PH2, RL2, RH2)
    for copy in second:
        copy.wait_recv()

    def unpack_rhs(l, carry):
        store_rim(Q0, l, rim_tile(RL2[...], RH2[...], l - 1))
        return carry

    lax.fori_loop(1, LV + 1, unpack_rhs, 0)

    shift = storage[0]
    scale = 1.0 / SHIFT

    def apply(q_ref, emit, sums):
        def level(l, carry):
            down, totals = carry
            v = q_ref[l]
            total, up = flow(q_ref, l, v, down)
            return up, emit(l, v, total, totals)

        first_down = KZ[0] * (zero - q_ref[1])
        none = tuple(jnp.zeros((8, 128), F32) for _ in range(sums))
        return lax.fori_loop(1, LV + 1, level, (first_down, none))[1]

    def emit0(l, v, total, sums):
        w = shift * v + total
        Q1[l] = (total * scale - v) * mask
        wi = w[0:RX, 0:CY]
        W0[l - 1] = wi
        return (sums[0] + fold(wi * v[0:RX, 0:CY]), sums[1] + fold(wi * wi))

    def emit1(l, v, total, sums):
        w = shift * v + total
        Q2[l] = (2.0 * (total * scale - v) - Q0[l]) * mask
        wi = w[0:RX, 0:CY]
        W1[l - 1] = wi
        return (
            sums[0] + fold(wi * Q0[l, 0:RX, 0:CY]),
            sums[1] + fold(wi * W0[l - 1]),
            sums[2] + fold(wi * wi),
        )

    def emit2(l, v, total, sums):
        wi = (shift * v + total)[0:RX, 0:CY]
        return (
            sums[0] + fold(wi * Q0[l, 0:RX, 0:CY]),
            sums[1] + fold(wi * W0[l - 1]),
            sums[2] + fold(wi * W1[l - 1]),
            sums[3] + fold(wi * wi),
        )

    b0, m00 = apply(Q0, emit0, 2)
    b1, m01, m11 = apply(Q1, emit1, 3)
    b2, m02, m12, m22 = apply(Q2, emit2, 4)
    one_lane = lax.broadcasted_iota(jnp.int32, (1, 128), 1)
    packed = jnp.zeros((1, 128), F32)
    for i, part in enumerate((b0, m00, b1, m01, m11, b2, m02, m12, m22)):
        packed = jnp.where(one_lane == i, jnp.sum(part, keepdims=True), packed)
    me = gx * 8 + gy
    ROW[0:1, :] = packed
    GATH[pl.ds(me, 1), :] = packed
    for peer in peers:
        pltpu.make_async_remote_copy(
            src_ref=ROW.at[pl.ds(0, 1)],
            dst_ref=GATH.at[pl.ds(me, 1)],
            send_sem=lsem.at[5],
            recv_sem=lsem.at[6],
            device_id=peer,
            device_id_type=MESH,
        ).start()
    all_rows = GATH.at[pl.ds(0, len(peers))]
    pltpu.make_async_copy(all_rows, all_rows, lsem.at[6]).wait()
    totals = jnp.sum(GATH[...], axis=0, keepdims=True)

    def at(i):
        return jnp.sum(jnp.where(one_lane == i, totals, 0.0), axis=1, keepdims=True)

    b0, m00, b1, m01, m11, b2, m02, m12, m22 = [at(i) for i in range(9)]
    l10, l20 = m01 / m00, m02 / m00
    d1 = m11 - m01 * l10
    e1 = m12 - m02 * l10
    l21 = e1 / d1
    d2 = m22 - m02 * l20 - e1 * l21
    z1 = b1 - l10 * b0
    z2 = b2 - l20 * b0 - l21 * z1
    y2 = z2 / d2
    y1 = z1 / d1 - l21 * y2
    y0 = b0 / m00 - l10 * y1 - l20 * y2

    def update(l, carry):
        out[0, l] = (
            S[l + 1, 0:RX, 0:CY]
            + y0 * Q0[l + 1, 0:RX, 0:CY]
            + y1 * Q1[l + 1, 0:RX, 0:CY]
            + y2 * Q2[l + 1, 0:RX, 0:CY]
        )
        return carry

    lax.fori_loop(0, LV, update, 0)
    pltpu.make_async_copy(all_rows, all_rows, lsem.at[5]).wait()
    for copy in sends:
        copy.wait_send()


def body(*args):
    any_spec = pl.BlockSpec(memory_space=pl.ANY)
    smem = pl.BlockSpec(memory_space=pltpu.SMEM)
    vmem = pl.BlockSpec(memory_space=pltpu.VMEM)
    field = pltpu.VMEM((LV + 2, EX, EY), F32)
    own = pltpu.VMEM((LV, RX, CY), F32)
    plane = pltpu.VMEM((RX, CY), F32)
    pack = pltpu.VMEM((RX, 128), F32)
    landing = pltpu.VMEM((EX, 128), F32)
    return pl.pallas_call(
        kernel,
        out_shape=(
            jax.ShapeDtypeStruct((1, LV, RX, CY), F32),
            jax.ShapeDtypeStruct((1, RX, CY), F32),
        ),
        in_specs=[any_spec, any_spec, smem, any_spec, any_spec, smem, smem, smem, any_spec],
        out_specs=(vmem, vmem),
        scratch_shapes=[
            field,
            field,
            field,
            field,
            field,
            field,
            field,
            field,
            own,
            own,
            pltpu.VMEM((NS, RX, CY), F32),
            plane,
            pltpu.VMEM((RX, CY), jnp.int32),
            pltpu.VMEM((CY, PATCH), F32),
            pltpu.VMEM((2 + 2 * NS, RX, CY), F32),
            plane,
            pltpu.VMEM((EX, EY), F32),
            pack,
            pack,
            landing,
            landing,
            pack,
            pack,
            landing,
            landing,
            pltpu.VMEM((8, 128), F32),
            pltpu.VMEM((64, 128), F32),
            pltpu.SemaphoreType.DMA((7,)),
            pltpu.SemaphoreType.DMA((24,)),
            pltpu.SemaphoreType.DMA((24,)),
        ],
        compiler_params=pltpu.CompilerParams(
            collective_id=0, has_side_effects=True, vmem_limit_bytes=40 * 1024 * 1024
        ),
    )(*args)


def solution(mesh):
    in_specs = (
        P("comp", None, "gx", "gy"),
        P("comp", None, "gx", "gy"),
        P("comp"),
        P("comp", "gx", "gy"),
        P("comp", "gx", "gy"),
        P(),
        P(),
        P("comp", "gx"),
        P("comp", "gy", None),
    )
    out_specs = (P("comp", None, "gx", "gy"), P("comp", "gx", "gy"))
    return jax.shard_map(body, mesh=mesh, in_specs=in_specs, out_specs=out_specs, check_vma=False)
```

time: 1810 us -> 75.7 us (0.04)
  blocking collectives: 1630 us -> 0 us
  Pallas kernels: 0 us -> 66.8 us
  other arithmetic: 64.2 us -> 0 us
  starting transfers between devices: 49.1 us -> 0 us
  local copies, waits for them, and re-layouts: 41 us -> 7.17 us
    psum x10 -> x0, blocking collectives: 1630 us -> none  [the longest x9 1470 us: inner(): return lax.psum(jnp.sum(a * b), ('gx', 'gy'))]
    pallas_call x0 -> x1, Pallas kernels: none -> 66.8 us  [body(): pl.pallas_call(kernel, out_shape=(jax.ShapeDtypeStruct((1, LV, RX, CY), F...]
    ppermute x17 -> x0, starting transfers between devices: 49.1 us -> none  [the longest x8 25.9 us: extended(): lax.ppermute(lax.slice_in_dim(block, block.shape[dim] - width, None, axis...]
    reduce_sum x11 -> x0, other arithmetic: 39.2 us -> none  [the longest x9 33.5 us: inner(): return lax.psum(jnp.sum(a * b), ('gx', 'gy'))]
  transfers between devices with their start and end apart: 17 -> 0, of which waited for: 6 -> 0; matrix products, arithmetic and copies ran while one was open for 2% -> 0% of each run, Pallas kernels for 0% -> 0%
where the time goes in v1:
time: 75.7 us; the launch traced here: 75.3 us
  Pallas kernels  66.8 us (88%)
  local copies, waits for them, and re-layouts  7.17 us (9%)
  between operations  1.31 us (2%)
    pallas_call x1, Pallas kernels, body(): pl.pallas_call(kernel, out_shape=(jax.ShapeDtypeStruct((1, LV, RX, CY), F...  66.8 us
    unnamed x16, local copies, waits for them, and re-layouts  7.17 us

profile of v1, /device:TPU:1, one launch (start us, length us, event | category | flops | bytes accessed | tf_op | source)
XLA Modules:
  0.0 75.3 jit_solution(14147359932190218722)
XLA Ops:
  0.6 0.0 copy-start.3
  1.3 0.8 %copy.11.ptab = f32[16,2]{1,0:T(8,128)S(1)} copy(f32[16,2]{0,1:T(2,128)} %param.14) | data formatting | bytes 256 | tf_op args[5]
  2.0 0.0 copy-start.5
  2.1 0.8 %copy.12.lw = f32[2,16,6]{2,1,0:T(8,128)S(1)} copy(f32[2,16,6]{1,0,2:T(2,128)} %param.15) | data formatting | bytes 1536 | tf_op args[6]
  2.8 0.0 copy-done.3
  2.8 0.0 copy-done.5
  2.8 0.0 copy-start
  2.9 1.2 %copy-done = f32[1,30,32,256]{3,2,1,0:T(8,128)S(1)} copy-done((f32[1,30,32,256]{3,2,1,0:T(8,128)S(1)}, f32[1,30,32,256]{3,2,1,0:T(8,128)}, u32[]{:S(2)}) %copy-start) | copy-done | bytes 983064
  4.0 0.0 copy-start.1
  4.0 1.2 %copy-done.1 = f32[1,30,32,256]{3,2,1,0:T(8,128)S(1)} copy-done((f32[1,30,32,256]{3,2,1,0:T(8,128)S(1)}, f32[1,30,32,256]{3,2,1,0:T(8,128)}, u32[]{:S(2)}) %copy-start.1) | copy-done | bytes 983064
  5.2 0.0 copy-start.2
  5.3 0.9 %copy-done.2 = f32[1,256,128]{2,1,0:T(8,128)S(1)} copy-done((f32[1,256,128]{2,1,0:T(8,128)S(1)}, f32[1,256,128]{2,1,0:T(8,128)}, u32[]{:S(2)}) %copy-start.2) | copy-done | bytes 131096
  6.2 0.0 copy-start.4
  6.2 0.8 %copy-done.4 = s32[1,32,256]{2,1,0:T(8,128)S(1)} copy-done((s32[1,32,256]{2,1,0:T(8,128)S(1)}, s32[1,32,256]{2,1,0:T(8,128)}, u32[]{:S(2)}) %copy-start.4) | copy-done | bytes 32792
  6.9 66.8 %shard_map.104 = (f32[1,30,32,256]{3,2,1,0:T(8,128)S(1)}, f32[1,32,256]{2,1,0:T(8,128)S(1)}) custom-call(f32[1,30,32,256]{3,2,1,0:T(8,128)S(1)} %copy-done, f32[1,30,32,256]{3,2,1,0:T(8,128)S(1)} %copy-done.1, f32[1]{0:T(128)S(6)} %copy.15.storage, f32[1,32,256]{2,1,0:T(8,128)S(1)} %copy-done.3, s32[1,32,256]{2,1,0:T(8,128)S(1)} %copy-done.4, ...), custom_call_target="tpu_custom_call" | custom-call | tf_op jit(solution)/shard_map/pallas_call | solution.py:440
  73.8 0.9 %copy.16 = f32[1,30,32,256]{3,2,1,0:T(8,128)} copy(f32[1,30,32,256]{3,2,1,0:T(8,128)S(1)} %get-tuple-element.4) | data formatting | bytes 1966080
  74.7 0.6 copy.17
Async XLA Ops:
  0.6 2.2 %copy-start.3 = (f32[1,32,256]{2,1,0:T(8,128)S(1)}, f32[1,32,256]{2,1,0:T(8,128)}, u32[]{:S(2)}) copy-start(f32[1,32,256]{2,1,0:T(8,128)} %surface.1) | copy-start | bytes 98308
  2.0 0.8 %copy-start.5 = (s32[1,32]{1,0:T(1,128)S(1)}, s32[1,32]{1,0:T(1,128)}, u32[]{:S(2)}) copy-start(s32[1,32]{1,0:T(1,128)} %rows.1) | copy-start | bytes 388
  2.8 1.2 %copy-start = (f32[1,30,32,256]{3,2,1,0:T(8,128)S(1)}, f32[1,30,32,256]{3,2,1,0:T(8,128)}, u32[]{:S(2)}) copy-start(f32[1,30,32,256]{3,2,1,0:T(8,128)} %state.1) | copy-start | bytes 2949124
  4.0 1.2 %copy-start.1 = (f32[1,30,32,256]{3,2,1,0:T(8,128)S(1)}, f32[1,30,32,256]{3,2,1,0:T(8,128)}, u32[]{:S(2)}) copy-start(f32[1,30,32,256]{3,2,1,0:T(8,128)} %conduct.1) | copy-start | bytes 2949124
  5.2 0.9 %copy-start.2 = (f32[1,256,128]{2,1,0:T(8,128)S(1)}, f32[1,256,128]{2,1,0:T(8,128)}, u32[]{:S(2)}) copy-start(f32[1,256,128]{2,1,0:T(8,128)} %rw_in.1) | copy-start | bytes 393220
  6.2 0.8 %copy-start.4 = (s32[1,32,256]{2,1,0:T(8,128)S(1)}, s32[1,32,256]{2,1,0:T(8,128)}, u32[]{:S(2)}) copy-start(s32[1,32,256]{2,1,0:T(8,128)} %kinds_in.1) | copy-start | bytes 98308

commit v2 on v1

v2 whole, which is shorter than its diff:
```python
import jax
import jax.numpy as jnp
from jax import lax
from jax.experimental import pallas as pl
from jax.experimental.pallas import tpu as pltpu
from jax.sharding import PartitionSpec as P

MESH = pl.DeviceIdType.MESH
F32 = jnp.float32
NS = 6
PATCH = 128
PLANTS = 16
LV = 30
RX = 32
CY = 256
RIM = 3
TILES = 3
EX = 48
LOW, HIGH = 8, 40
OWN_ROWS = slice(LOW, HIGH)
EDGE = 96
SHIFT = 7.0
HP = lax.Precision.HIGHEST


def shifted(rows, by):
    return slice(rows.start + by, rows.stop + by)


def fold(x):
    return (x[0:8] + x[8:16]) + (x[16:24] + x[24:32])


def far_first():
    offsets = []
    for dx in range(4):
        for dh in range(2):
            for dz in range(4):
                for co in range(2):
                    if (dx, dh, dz, co) != (0, 0, 0, 0):
                        hops = min(dx, 4 - dx) + 2 * dh + min(dz, 4 - dz)
                        offsets.append((hops, co, dx, dh, dz))
    return [(dx, dh, dz, co) for _, co, dx, dh, dz in sorted(offsets, reverse=True)]


def kernel(
    state,
    conduct,
    storage,
    surface,
    kinds_in,
    ptab,
    lw,
    rows,
    rw_in,
    out,
    flux_out,
    S,
    K,
    KX,
    KY,
    KYM,
    KZ,
    Q0,
    Q1,
    Q2,
    W0,
    W1,
    PART,
    SURF,
    KINDS,
    RW,
    TAB,
    OWN,
    PL1,
    PH1,
    RL1,
    RH1,
    PL2,
    PH2,
    RL2,
    RH2,
    ROW,
    GATH,
    lsem,
    ssem,
    rsem,
):
    c, gx, gy = lax.axis_index("comp"), lax.axis_index("gx"), lax.axis_index("gy")
    xp, xm = lax.rem(gx + 1, 8), lax.rem(gx + 7, 8)
    yp, ym = lax.rem(gy + 1, 8), lax.rem(gy + 7, 8)
    partner = (1 - c, gx, gy)

    local = []
    for src, dst in ((state, S), (conduct, K)):
        for t in range(2):
            local.append(
                pltpu.make_async_copy(
                    src.at[0, :, :, pl.ds(128 * t, 128)],
                    dst.at[t, :, pl.ds(LOW, RX), :],
                    lsem.at[len(local)],
                )
            )
    for src, dst in ((surface, SURF), (kinds_in, KINDS), (rw_in, RW)):
        local.append(pltpu.make_async_copy(src.at[0], dst, lsem.at[len(local)]))
    for copy in local:
        copy.start()

    peers = [
        (
            c,
            lax.rem(gx // 2 + dx, 4) * 2 + lax.rem(gx + dh, 2),
            lax.rem(gy // 2 + dz, 4) * 2 + lax.rem(gy + co, 2),
        )
        for dx, dh, dz, co in far_first()
    ]
    barrier = pltpu.get_barrier_semaphore()
    for peer in peers + [partner]:
        pl.semaphore_signal(barrier, inc=1, device_id=peer, device_id_type=MESH)

    for copy in local[:4]:
        copy.wait()
    lane = lax.broadcasted_iota(jnp.int32, (RX, 128), 1)
    blank = jnp.zeros((RX, 128), F32)

    def edges(value0, value1, l, low, high):
        own = (lane >= RIM * l) & (lane < RIM * l + RIM)
        low = jnp.where(own, pltpu.roll(value0, RIM * l, 1), low)
        high = jnp.where(own, pltpu.roll(value1, RIM * l + RIM, 1), high)
        return low, high

    low, high = blank, blank
    for l in range(LV):
        s = [S[t, l, OWN_ROWS, :] for t in range(2)]
        k = [K[t, l, OWN_ROWS, :] * (1.0 + 0.5 * jnp.tanh(s[t])) for t in range(2)]
        for t in range(2):
            K[t, l, OWN_ROWS, :] = k[t]
        low, high = edges(k[0], k[1], l, low, high)
        own = lane == EDGE + l
        low = jnp.where(own, pltpu.roll(s[0], EDGE + l, 1), low)
        high = jnp.where(own, pltpu.roll(s[1], EDGE + 1 + l, 1), high)
    PL1[...] = low
    PH1[...] = high

    pl.semaphore_wait(barrier, len(peers) + 1)

    sends = []

    def send(src, dst, device):
        i = len(sends)
        copy = pltpu.make_async_remote_copy(
            src_ref=src,
            dst_ref=dst,
            send_sem=ssem.at[i],
            recv_sem=rsem.at[i],
            device_id=device,
            device_id_type=MESH,
        )
        copy.start()
        sends.append(copy)
        return copy

    own_tiles, own_levels = pl.ds(0, 2), pl.ds(0, LV)

    def send_rows(ref, width):
        return [
            send(
                ref.at[own_tiles, own_levels, pl.ds(LOW, width), :],
                ref.at[own_tiles, own_levels, pl.ds(HIGH, width), :],
                (c, xm, gy),
            ),
            send(
                ref.at[own_tiles, own_levels, pl.ds(HIGH - width, width), :],
                ref.at[own_tiles, own_levels, pl.ds(LOW - width, width), :],
                (c, xp, gy),
            ),
        ]

    def send_packs(low_pack, high_pack, from_low, from_high):
        made = [
            send(low_pack, from_high.at[pl.ds(LOW, RX)], (c, gx, ym)),
            send(high_pack, from_low.at[pl.ds(LOW, RX)], (c, gx, yp)),
        ]
        for pack, landing, y in ((low_pack, from_high, ym), (high_pack, from_low, yp)):
            made.append(send(pack.at[pl.ds(0, RIM)], landing.at[pl.ds(HIGH, RIM)], (c, xm, y)))
            made.append(
                send(pack.at[pl.ds(RX - RIM, RIM)], landing.at[pl.ds(LOW - RIM, RIM)], (c, xp, y))
            )
        return made

    levels_copy = send(state.at[0, pl.ds(0, NS)], PART, partner)
    first = send_rows(S, 1) + send_rows(K, RIM) + send_packs(PL1, PH1, RL1, RH1)

    for copy in local[4:]:
        copy.wait()

    def look_up(r, carry):
        at = pl.ds(pl.multiple_of(r * 8, 8), 8)
        below = pl.ds(pl.multiple_of(r * 8 + LOW, 8), 8)
        kinds = KINDS[at, :]
        found = [jnp.zeros((8, CY), F32) for _ in range(2 + 2 * NS)]
        for p in range(PLANTS):
            hit = kinds == p
            values = [ptab[0, p], ptab[1, p]]
            values += [lw[l, c, p] for l in range(NS)] + [lw[l, 1 - c, p] for l in range(NS)]
            found = [jnp.where(hit, v, f) for v, f in zip(values, found)]
        for t, f in enumerate(found):
            TAB[t, at, :] = f
        own = jnp.zeros((8, CY), F32)
        for l in range(NS):
            s = jnp.concatenate([S[0, l, below, :], S[1, l, below, :]], axis=1)
            own = own + found[2 + l] * s
        OWN[at, :] = own
        return carry

    lax.fori_loop(0, RX // 8, look_up, 0)
    pick_row = lax.broadcasted_iota(jnp.int32, (RX, RX), 0)
    pick_col = lax.broadcasted_iota(jnp.int32, (RX, RX), 1)
    wanted = jnp.zeros((RX, RX), jnp.int32)
    for x in range(RX):
        wanted = jnp.where(pick_row == x, rows[0, x], wanted)
    picker = jnp.where(wanted == pick_col, 1.0, 0.0).astype(F32)

    for copy in first:
        copy.wait_recv()

    row = lax.broadcasted_iota(jnp.int32, (EX, 128), 0)
    row_ok = (
        ((row >= LOW) & (row < HIGH))
        | ((row >= LOW - RIM) & (row < LOW) & (gx > 0))
        | ((row >= HIGH) & (row < HIGH + RIM) & (gx < 7))
    )

    def clean_packs(from_low, from_high):
        from_low[...] = jnp.where(row_ok & (gy > 0), from_low[...], 0.0)
        from_high[...] = jnp.where(row_ok & (gy < 7), from_high[...], 0.0)

    def clear_rows(ref, tiles, width):
        @pl.when(gx == 0)
        def _():
            for t in range(tiles):
                ref[t, :, LOW - width : LOW, :] = jnp.zeros((LV, width, 128), F32)

        @pl.when(gx == 7)
        def _():
            for t in range(tiles):
                ref[t, :, HIGH : HIGH + width, :] = jnp.zeros((LV, width, 128), F32)

    clean_packs(RL1, RH1)
    clear_rows(S, 2, 1)
    clear_rows(K, 2, RIM)

    def lanes_of(rows):
        return lax.broadcasted_iota(jnp.int32, (rows.stop - rows.start, 128), 1)

    def fill_rim(ref, from_low, from_high, rows):
        lane_at = lanes_of(rows)
        for l in range(LV):
            right = pltpu.roll(from_high[rows, :], (128 - RIM * l) % 128, 1)
            left = pltpu.roll(from_low[rows, :], (125 - RIM * l) % 128, 1)
            ref[2, l, rows, :] = jnp.where(
                lane_at < RIM, right, jnp.where(lane_at >= 128 - RIM, left, 0.0)
            )

    wide = slice(LOW - RIM, HIGH + RIM)
    fill_rim(K, RL1, RH1, wide)

    near = slice(LOW - 2, HIGH + 2)
    pair = slice(LOW - 3, HIGH + 2)
    lane_near = lanes_of(near)
    below = [None] * TILES
    for l in range(LV + 1):
        k = [K[t, l, near, :] for t in range(TILES)] if l < LV else None
        for t in range(TILES):
            if l == 0:
                KZ[t, l, near, :] = 0.5 * k[t]
            elif l == LV:
                KZ[t, l, near, :] = 0.5 * below[t]
            else:
                KZ[t, l, near, :] = 0.5 * (below[t] + k[t])
        if l == LV:
            break
        below = k
        high_side = [pltpu.roll(x, 127, 1) for x in k]
        low_side = [pltpu.roll(x, 1, 1) for x in k]
        for t in range(TILES):
            KX[t, l, pair, :] = 0.5 * (K[t, l, pair, :] + K[t, l, shifted(pair, 1), :])
            right = jnp.where(lane_near == 127, high_side[(t + 1) % 3], high_side[t])
            left = jnp.where(lane_near == 0, low_side[(t + 2) % 3], low_side[t])
            KY[t, l, near, :] = 0.5 * (k[t] + right)
            KYM[t, l, near, :] = 0.5 * (k[t] + left)

    def flow(ref, l, t, x, rows, right, left):
        total = KX[t, l, rows, :] * (x - ref[t, l, shifted(rows, 1), :])
        before = shifted(rows, -1)
        total = total + KX[t, l, before, :] * (x - ref[t, l, before, :])
        total = total + KY[t, l, rows, :] * (x - right)
        total = total + KYM[t, l, rows, :] * (x - left)
        up = x if l == LV - 1 else x - ref[t, l + 1, rows, :]
        down = x if l == 0 else x - ref[t, l - 1, rows, :]
        return total + (KZ[t, l + 1, rows, :] * up + KZ[t, l, rows, :] * down)

    first_lane, last_lane = lane == 0, lane == 127
    for l in range(LV):
        s = [S[t, l, OWN_ROWS, :] for t in range(2)]
        beyond = pltpu.roll(RH1[OWN_ROWS, :], 31 - l, 1)
        before = pltpu.roll(RL1[OWN_ROWS, :], 32 - l, 1)
        to_low = [pltpu.roll(x, 127, 1) for x in s] + [beyond]
        to_high = [pltpu.roll(x, 1, 1) for x in s] + [before]
        for t in range(2):
            right = jnp.where(last_lane, to_low[t + 1], to_low[t])
            left = jnp.where(first_lane, to_high[(t + 2) % 3], to_high[t])
            Q0[t, l, OWN_ROWS, :] = -flow(S, l, t, s[t], OWN_ROWS, right, left)

    levels_copy.wait_recv()
    received = PART[...].reshape(NS * RX, CY)
    mixed = jnp.concatenate(
        [
            lax.dot_general(
                received[:, b : b + PATCH],
                RW[b : b + PATCH, :],
                (((1,), (1,)), ((), ())),
                precision=HP,
                preferred_element_type=F32,
            )
            for b in range(0, CY, PATCH)
        ],
        axis=1,
    )
    other = jnp.zeros((RX, CY), F32)
    for l in range(NS):
        remapped = jnp.dot(
            picker, mixed[l * RX : (l + 1) * RX], precision=HP, preferred_element_type=F32
        )
        other = other + TAB[2 + NS + l] * remapped
    own = OWN[...]
    is_air = c == 0
    air = jnp.where(is_air, own, other)
    soil = jnp.where(is_air, other, own)
    flux = TAB[0] * (TAB[1] * soil - air)
    flux_out[0] = flux
    signed = jnp.where(is_air, flux, -flux)
    for l in range(NS):
        top = signed * TAB[2 + l]
        if l == 0:
            top = top + SURF[...]
        for t in range(2):
            Q0[t, l, OWN_ROWS, :] = Q0[t, l, OWN_ROWS, :] + top[:, 128 * t : 128 * t + 128]

    low, high = blank, blank
    for l in range(LV):
        low, high = edges(Q0[0, l, OWN_ROWS, :], Q0[1, l, OWN_ROWS, :], l, low, high)
    PL2[...] = low
    PH2[...] = high
    second = send_rows(Q0, RIM) + send_packs(PL2, PH2, RL2, RH2)
    for copy in second:
        copy.wait_recv()
    clean_packs(RL2, RH2)
    clear_rows(Q0, 2, RIM)
    fill_rim(Q0, RL2, RH2, wide)

    shift = storage[0]
    scale = 1.0 / SHIFT

    def apply(q_ref, rows, tiles, emit):
        lane_at = lanes_of(rows)
        for l in range(LV):
            x = [q_ref[t, l, rows, :] for t in range(TILES)]
            to_low = [pltpu.roll(v, 127, 1) for v in x]
            to_high = [pltpu.roll(v, 1, 1) for v in x]
            for t in range(tiles):
                right = jnp.where(lane_at == 127, to_low[(t + 1) % 3], to_low[t])
                left = jnp.where(lane_at == 0, to_high[(t + 2) % 3], to_high[t])
                emit(l, t, x[t], flow(q_ref, l, t, x[t], rows, right, left), rows)

    rim_ok = ((lane_near < RIM) & (gy < 7)) | ((lane_near >= 128 - RIM) & (gy > 0))
    rim_mask = jnp.where(rim_ok, 1.0, 0.0).astype(F32)

    def emit0(l, t, x, total, rows):
        q = total * scale - x
        if t < 2:
            W0[t, l, rows, :] = shift * x + total
        else:
            q = q * rim_mask
        Q1[t, l, rows, :] = q

    def emit1(l, t, x, total, rows):
        q = 2.0 * (total * scale - x) - Q0[t, l, rows, :]
        if t < 2:
            W1[t, l, rows, :] = shift * x + total
        else:
            q = q * rim_mask[0 : rows.stop - rows.start]
        Q2[t, l, rows, :] = q

    sums = [jnp.zeros((8, 128), F32) for _ in range(9)]

    def emit2(l, t, x, total, rows):
        w2 = shift * x + total
        w0, w1, q0 = W0[t, l, rows, :], W1[t, l, rows, :], Q0[t, l, rows, :]
        products = (w0 * q0, w0 * w0, w1 * q0, w1 * w0, w1 * w1, w2 * q0, w2 * w0, w2 * w1, w2 * w2)
        for i, product in enumerate(products):
            sums[i] = sums[i] + fold(product)

    apply(Q0, near, TILES, emit0)
    clear_rows(Q1, TILES, 2)
    apply(Q1, slice(LOW - 1, HIGH + 1), TILES, emit1)
    clear_rows(Q2, TILES, 1)
    apply(Q2, OWN_ROWS, 2, emit2)

    one_lane = lax.broadcasted_iota(jnp.int32, (1, 128), 1)
    packed = jnp.zeros((1, 128), F32)
    for i, part in enumerate(sums):
        packed = jnp.where(one_lane == i, jnp.sum(part, keepdims=True), packed)
    me = gx * 8 + gy
    ROW[0:1, :] = packed
    GATH[pl.ds(me, 1), :] = packed
    for peer in peers:
        pltpu.make_async_remote_copy(
            src_ref=ROW.at[pl.ds(0, 1)],
            dst_ref=GATH.at[pl.ds(me, 1)],
            send_sem=lsem.at[7],
            recv_sem=lsem.at[8],
            device_id=peer,
            device_id_type=MESH,
        ).start()
    all_rows = GATH.at[pl.ds(0, len(peers))]
    pltpu.make_async_copy(all_rows, all_rows, lsem.at[8]).wait()
    totals = jnp.sum(GATH[...], axis=0, keepdims=True)
    def at(i):
        return jnp.sum(jnp.where(one_lane == i, totals, 0.0), axis=1, keepdims=True)

    b0, m00, b1, m01, m11, b2, m02, m12, m22 = [at(i) for i in range(9)]
    l10, l20 = m01 / m00, m02 / m00
    d1 = m11 - m01 * l10
    e1 = m12 - m02 * l10
    l21 = e1 / d1
    d2 = m22 - m02 * l20 - e1 * l21
    z1 = b1 - l10 * b0
    z2 = b2 - l20 * b0 - l21 * z1
    y2 = z2 / d2
    y1 = z1 / d1 - l21 * y2
    y0 = b0 / m00 - l10 * y1 - l20 * y2

    for l in range(LV):
        for t in range(2):
            out[0, l, :, 128 * t : 128 * t + 128] = (
                S[t, l, OWN_ROWS, :]
                + y0 * Q0[t, l, OWN_ROWS, :]
                + y1 * Q1[t, l, OWN_ROWS, :]
                + y2 * Q2[t, l, OWN_ROWS, :]
            )
    pltpu.make_async_copy(all_rows, all_rows, lsem.at[7]).wait()
    for copy in sends:
        copy.wait_send()


def body(state, conduct, storage, surface, kinds, ptab, lw, rows, rw):
    hbm = pl.BlockSpec(memory_space=pltpu.HBM)
    smem = pl.BlockSpec(memory_space=pltpu.SMEM)
    vmem = pl.BlockSpec(memory_space=pltpu.VMEM)
    field = pltpu.VMEM((TILES, LV, EX, 128), F32)
    inner = pltpu.VMEM((2, LV, EX, 128), F32)
    plane = pltpu.VMEM((RX, CY), F32)
    pack = pltpu.VMEM((RX, 128), F32)
    landing = pltpu.VMEM((EX, 128), F32)
    return pl.pallas_call(
        kernel,
        out_shape=(
            jax.ShapeDtypeStruct((1, LV, RX, CY), F32),
            jax.ShapeDtypeStruct((1, RX, CY), F32),
        ),
        in_specs=[hbm, hbm, smem, hbm, hbm, smem, smem, smem, hbm],
        out_specs=(vmem, vmem),
        scratch_shapes=[
            inner,
            field,
            field,
            field,
            field,
            pltpu.VMEM((TILES, LV + 1, EX, 128), F32),
            field,
            field,
            field,
            inner,
            inner,
            pltpu.VMEM((NS, RX, CY), F32),
            plane,
            pltpu.VMEM((RX, CY), jnp.int32),
            pltpu.VMEM((CY, PATCH), F32),
            pltpu.VMEM((2 + 2 * NS, RX, CY), F32),
            plane,
            pack,
            pack,
            landing,
            landing,
            pack,
            pack,
            landing,
            landing,
            pltpu.VMEM((8, 128), F32),
            pltpu.VMEM((64, 128), F32),
            pltpu.SemaphoreType.DMA((9,)),
            pltpu.SemaphoreType.DMA((24,)),
            pltpu.SemaphoreType.DMA((24,)),
        ],
        compiler_params=pltpu.CompilerParams(
            collective_id=0, has_side_effects=True, vmem_limit_bytes=63 * 1024 * 1024
        ),
    )(state, conduct, storage, surface, kinds, ptab.T, jnp.transpose(lw, (2, 0, 1)), rows, rw)


def solution(mesh):
    in_specs = (
        P("comp", None, "gx", "gy"),
        P("comp", None, "gx", "gy"),
        P("comp"),
        P("comp", "gx", "gy"),
        P("comp", "gx", "gy"),
        P(),
        P(),
        P("comp", "gx"),
        P("comp", "gy", None),
    )
    out_specs = (P("comp", None, "gx", "gy"), P("comp", "gx", "gy"))
    return jax.shard_map(body, mesh=mesh, in_specs=in_specs, out_specs=out_specs, check_vma=False)
```

time: 75.7 us -> 49 us (0.65)
  Pallas kernels: 66.8 us -> 44.6 us
  local copies, waits for them, and re-layouts: 7.17 us -> 2.87 us
    pallas_call x1, Pallas kernels: 66.8 us -> 44.6 us  [body(): pl.pallas_call(kernel, out_shape=(jax.ShapeDtypeStruct((1, LV, RX, CY), F...]
    unnamed x16 -> x4, local copies, waits for them, and re-layouts: 7.17 us -> 2.87 us
where the time goes in v2:
time: 49 us; the launch traced here: 48.8 us
  Pallas kernels  44.6 us (91%)
  local copies, waits for them, and re-layouts  2.87 us (6%)
  between operations  1.29 us (3%)
    pallas_call x1, Pallas kernels, body(): pl.pallas_call(kernel, out_shape=(jax.ShapeDtypeStruct((1, LV, RX, CY), F...  44.6 us
    unnamed x4, local copies, waits for them, and re-layouts  2.87 us

profile of v2, /device:TPU:1, one launch (start us, length us, event | category | flops | bytes accessed | tf_op | source)
XLA Modules:
  0.0 48.8 jit_solution(3655321714379212283)
XLA Ops:
  1.3 44.6 %shard_map.104 = (f32[1,30,32,256]{3,2,1,0:T(8,128)}, f32[1,32,256]{2,1,0:T(8,128)}) custom-call(f32[1,30,32,256]{3,2,1,0:T(8,128)} %state.1, f32[1,30,32,256]{3,2,1,0:T(8,128)} %conduct.1, f32[1]{0:T(128)S(6)} %copy.13.storage, f32[1,32,256]{2,1,0:T(8,128)} %surface.1, s32[1,32,256]{2,1,0:T(8,128)} %kinds_in.1, f32[2,16]{1,0:T(2,128)} %bitcast.3, ...), custom_call_target="tpu_custom_call" | custom-call | tf_op jit(solution)/shard_map/pallas_call | solution.py:466
  45.9 0.0 copy-start
  45.9 2.3 %copy.14 = f32[1,30,32,256]{3,2,1,0:T(8,128)} copy(f32[1,30,32,256]{3,2,1,0:T(8,128)} %get-tuple-element.4) | data formatting | bytes 1966080
  48.2 0.0 copy-done
  48.2 0.6 %copy.15 = f32[1,32,256]{2,1,0:T(8,128)} copy(f32[1,32,256]{2,1,0:T(8,128)S(1)} %copy-done) | data formatting | bytes 65536
Async XLA Ops:
  45.9 2.3 %copy-start = (f32[1,32,256]{2,1,0:T(8,128)S(1)}, f32[1,32,256]{2,1,0:T(8,128)}, u32[]{:S(2)}) copy-start(f32[1,32,256]{2,1,0:T(8,128)} %get-tuple-element.5) | copy-start | bytes 98308

commit v3 on v2

--- a/solution.py
+++ b/solution.py
@@ -80,6 +80,10 @@
     PH2,
     RL2,
     RH2,
+    PL3,
+    PH3,
+    RL3,
+    RH3,
     ROW,
     GATH,
     lsem,
@@ -160,27 +164,31 @@
         sends.append(copy)
         return copy
 
-    own_tiles, own_levels = pl.ds(0, 2), pl.ds(0, LV)
-
-    def send_rows(ref, width):
+    own_tiles = pl.ds(0, 2)
+
+    def send_rows(ref, skip, width, levels):
+        at, n = pl.ds(*levels), pl.ds
         return [
             send(
-                ref.at[own_tiles, own_levels, pl.ds(LOW, width), :],
-                ref.at[own_tiles, own_levels, pl.ds(HIGH, width), :],
+                ref.at[own_tiles, at, n(LOW + skip, width), :],
+                ref.at[own_tiles, at, n(HIGH + skip, width), :],
                 (c, xm, gy),
             ),
             send(
-                ref.at[own_tiles, own_levels, pl.ds(HIGH - width, width), :],
-                ref.at[own_tiles, own_levels, pl.ds(LOW - width, width), :],
+                ref.at[own_tiles, at, n(HIGH - skip - width, width), :],
+                ref.at[own_tiles, at, n(LOW - skip - width, width), :],
                 (c, xp, gy),
             ),
         ]
 
     def send_packs(low_pack, high_pack, from_low, from_high):
-        made = [
+        return [
             send(low_pack, from_high.at[pl.ds(LOW, RX)], (c, gx, ym)),
             send(high_pack, from_low.at[pl.ds(LOW, RX)], (c, gx, yp)),
         ]
+
+    def send_corners(low_pack, high_pack, from_low, from_high):
+        made = []
         for pack, landing, y in ((low_pack, from_high, ym), (high_pack, from_low, yp)):
             made.append(send(pack.at[pl.ds(0, RIM)], landing.at[pl.ds(HIGH, RIM)], (c, xm, y)))
             made.append(
@@ -188,8 +196,10 @@
             )
         return made
 
+    every = (0, LV)
+    first = send_rows(S, 0, 1, every) + send_rows(K, 0, 1, every) + send_packs(PL1, PH1, RL1, RH1)
     levels_copy = send(state.at[0, pl.ds(0, NS)], PART, partner)
-    first = send_rows(S, 1) + send_rows(K, RIM) + send_packs(PL1, PH1, RL1, RH1)
+    rest = send_corners(PL1, PH1, RL1, RH1) + send_rows(K, 1, RIM - 1, every)
 
     for copy in local[4:]:
         copy.wait()
@@ -231,31 +241,36 @@
         | ((row >= HIGH) & (row < HIGH + RIM) & (gx < 7))
     )
 
-    def clean_packs(from_low, from_high):
-        from_low[...] = jnp.where(row_ok & (gy > 0), from_low[...], 0.0)
-        from_high[...] = jnp.where(row_ok & (gy < 7), from_high[...], 0.0)
-
-    def clear_rows(ref, tiles, width):
+    def clean_packs(from_low, from_high, spans):
+        for span in spans:
+            ok = row_ok[span]
+            from_low[span, :] = jnp.where(ok & (gy > 0), from_low[span, :], 0.0)
+            from_high[span, :] = jnp.where(ok & (gy < 7), from_high[span, :], 0.0)
+
+    def clear_rows(ref, tiles, skip, width, levels):
+        begin, count = levels
+        blank_rows = jnp.zeros((count, width, 128), F32)
+
         @pl.when(gx == 0)
         def _():
             for t in range(tiles):
-                ref[t, :, LOW - width : LOW, :] = jnp.zeros((LV, width, 128), F32)
+                ref[t, begin : begin + count, LOW - skip - width : LOW - skip, :] = blank_rows
 
         @pl.when(gx == 7)
         def _():
             for t in range(tiles):
-                ref[t, :, HIGH : HIGH + width, :] = jnp.zeros((LV, width, 128), F32)
-
-    clean_packs(RL1, RH1)
-    clear_rows(S, 2, 1)
-    clear_rows(K, 2, RIM)
+                ref[t, begin : begin + count, HIGH + skip : HIGH + skip + width, :] = blank_rows
+
+    clean_packs(RL1, RH1, (OWN_ROWS,))
+    clear_rows(S, 2, 0, 1, every)
+    clear_rows(K, 2, 0, 1, every)
 
     def lanes_of(rows):
         return lax.broadcasted_iota(jnp.int32, (rows.stop - rows.start, 128), 1)
 
-    def fill_rim(ref, from_low, from_high, rows):
+    def fill_rim(ref, from_low, from_high, rows, levels):
         lane_at = lanes_of(rows)
-        for l in range(LV):
+        for l in range(levels[0], levels[0] + levels[1]):
             right = pltpu.roll(from_high[rows, :], (128 - RIM * l) % 128, 1)
             left = pltpu.roll(from_low[rows, :], (125 - RIM * l) % 128, 1)
             ref[2, l, rows, :] = jnp.where(
@@ -263,32 +278,20 @@
             )
 
     wide = slice(LOW - RIM, HIGH + RIM)
-    fill_rim(K, RL1, RH1, wide)
-
     near = slice(LOW - 2, HIGH + 2)
-    pair = slice(LOW - 3, HIGH + 2)
     lane_near = lanes_of(near)
-    below = [None] * TILES
-    for l in range(LV + 1):
-        k = [K[t, l, near, :] for t in range(TILES)] if l < LV else None
-        for t in range(TILES):
-            if l == 0:
-                KZ[t, l, near, :] = 0.5 * k[t]
-            elif l == LV:
-                KZ[t, l, near, :] = 0.5 * below[t]
-            else:
-                KZ[t, l, near, :] = 0.5 * (below[t] + k[t])
-        if l == LV:
-            break
-        below = k
-        high_side = [pltpu.roll(x, 127, 1) for x in k]
-        low_side = [pltpu.roll(x, 1, 1) for x in k]
-        for t in range(TILES):
-            KX[t, l, pair, :] = 0.5 * (K[t, l, pair, :] + K[t, l, shifted(pair, 1), :])
-            right = jnp.where(lane_near == 127, high_side[(t + 1) % 3], high_side[t])
-            left = jnp.where(lane_near == 0, low_side[(t + 2) % 3], low_side[t])
-            KY[t, l, near, :] = 0.5 * (k[t] + right)
-            KYM[t, l, near, :] = 0.5 * (k[t] + left)
+
+    def vertical(t, l, rows):
+        if l == 0:
+            total = K[t, 0, rows, :]
+        elif l == LV:
+            total = K[t, LV - 1, rows, :]
+        else:
+            total = K[t, l - 1, rows, :] + K[t, l, rows, :]
+        KZ[t, l, rows, :] = 0.5 * total
+
+    def along_rows(t, l, rows):
+        KX[t, l, rows, :] = 0.5 * (K[t, l, rows, :] + K[t, l, shifted(rows, 1), :])
 
     def flow(ref, l, t, x, rows, right, left):
         total = KX[t, l, rows, :] * (x - ref[t, l, shifted(rows, 1), :])
@@ -301,16 +304,48 @@
         return total + (KZ[t, l + 1, rows, :] * up + KZ[t, l, rows, :] * down)
 
     first_lane, last_lane = lane == 0, lane == 127
-    for l in range(LV):
+
+    def beside(values, beyond, before, t):
+        to_low = [pltpu.roll(x, 127, 1) for x in values] + [beyond]
+        to_high = [pltpu.roll(x, 1, 1) for x in values] + [before]
+        right = jnp.where(last_lane, to_low[t + 1], to_low[t])
+        left = jnp.where(first_lane, to_high[(t + 2) % 3], to_high[t])
+        return right, left
+
+    def residual(l, start):
+        k = [K[t, l, OWN_ROWS, :] for t in range(2)]
         s = [S[t, l, OWN_ROWS, :] for t in range(2)]
-        beyond = pltpu.roll(RH1[OWN_ROWS, :], 31 - l, 1)
-        before = pltpu.roll(RL1[OWN_ROWS, :], 32 - l, 1)
-        to_low = [pltpu.roll(x, 127, 1) for x in s] + [beyond]
-        to_high = [pltpu.roll(x, 1, 1) for x in s] + [before]
+        k_beyond = pltpu.roll(RH1[OWN_ROWS, :], (127 - RIM * l) % 128, 1)
+        k_before = pltpu.roll(RL1[OWN_ROWS, :], (126 - RIM * l) % 128, 1)
+        s_beyond = pltpu.roll(RH1[OWN_ROWS, :], 31 - l, 1)
+        s_before = pltpu.roll(RL1[OWN_ROWS, :], 32 - l, 1)
         for t in range(2):
-            right = jnp.where(last_lane, to_low[t + 1], to_low[t])
-            left = jnp.where(first_lane, to_high[(t + 2) % 3], to_high[t])
+            if l == start:
+                vertical(t, l, OWN_ROWS)
+            if l + 1 != NS or start == NS:
+                vertical(t, l + 1, OWN_ROWS)
+            along_rows(t, l, slice(LOW - 1, HIGH))
+            right, left = beside(k, k_beyond, k_before, t)
+            KY[t, l, OWN_ROWS, :] = 0.5 * (k[t] + right)
+            KYM[t, l, OWN_ROWS, :] = 0.5 * (k[t] + left)
+            right, left = beside(s, s_beyond, s_before, t)
             Q0[t, l, OWN_ROWS, :] = -flow(S, l, t, s[t], OWN_ROWS, right, left)
+
+    def send_basis(levels, pack_low, pack_high, from_low, from_high):
+        low, high = blank, blank
+        for l in range(levels[0], levels[0] + levels[1]):
+            low, high = edges(Q0[0, l, OWN_ROWS, :], Q0[1, l, OWN_ROWS, :], l, low, high)
+        pack_low[...] = low
+        pack_high[...] = high
+        packs = (pack_low, pack_high, from_low, from_high)
+        return send_corners(*packs) + send_rows(Q0, 0, RIM, levels) + send_packs(*packs)
+
+    for l in range(NS, LV):
+        residual(l, NS)
+    deep = (NS, LV - NS)
+    deep_copies = send_basis(deep, PL2, PH2, RL2, RH2)
+    for l in range(NS):
+        residual(l, 0)
 
     levels_copy.wait_recv()
     received = PART[...].reshape(NS * RX, CY)
@@ -347,24 +382,48 @@
         for t in range(2):
             Q0[t, l, OWN_ROWS, :] = Q0[t, l, OWN_ROWS, :] + top[:, 128 * t : 128 * t + 128]
 
-    low, high = blank, blank
-    for l in range(LV):
-        low, high = edges(Q0[0, l, OWN_ROWS, :], Q0[1, l, OWN_ROWS, :], l, low, high)
-    PL2[...] = low
-    PH2[...] = high
-    second = send_rows(Q0, RIM) + send_packs(PL2, PH2, RL2, RH2)
-    for copy in second:
+    coupled = (0, NS)
+    coupled_copies = send_basis(coupled, PL3, PH3, RL3, RH3)
+
+    for copy in rest:
         copy.wait_recv()
-    clean_packs(RL2, RH2)
-    clear_rows(Q0, 2, RIM)
-    fill_rim(Q0, RL2, RH2, wide)
+    clean_packs(RL1, RH1, (slice(0, LOW), slice(HIGH, EX)))
+    clear_rows(K, 2, 1, RIM - 1, every)
+    fill_rim(K, RL1, RH1, wide, every)
+    for l in range(LV + 1):
+        for rows in (slice(LOW - 2, LOW), slice(HIGH, HIGH + 2)):
+            for t in range(2):
+                vertical(t, l, rows)
+        vertical(2, l, near)
+        if l == LV:
+            break
+        for t in range(2):
+            along_rows(t, l, slice(LOW - 3, LOW - 1))
+            along_rows(t, l, slice(HIGH, HIGH + 2))
+        along_rows(2, l, slice(LOW - 3, HIGH + 2))
+        for rows, tiles in ((slice(LOW - 2, LOW), (0, 1)), (slice(HIGH, HIGH + 2), (0, 1)), (near, (2,))):
+            lane_at = lanes_of(rows)
+            k = [K[t, l, rows, :] for t in range(TILES)]
+            for t in tiles:
+                beyond, before = pltpu.roll(k[(t + 1) % 3], 127, 1), pltpu.roll(k[(t + 2) % 3], 1, 1)
+                right = jnp.where(lane_at == 127, beyond, pltpu.roll(k[t], 127, 1))
+                left = jnp.where(lane_at == 0, before, pltpu.roll(k[t], 1, 1))
+                KY[t, l, rows, :] = 0.5 * (k[t] + right)
+                KYM[t, l, rows, :] = 0.5 * (k[t] + left)
+
+    def land_basis(copies, levels, from_low, from_high):
+        for copy in copies:
+            copy.wait_recv()
+        clean_packs(from_low, from_high, (slice(0, EX),))
+        clear_rows(Q0, 2, 0, RIM, levels)
+        fill_rim(Q0, from_low, from_high, wide, levels)
 
     shift = storage[0]
     scale = 1.0 / SHIFT
 
-    def apply(q_ref, rows, tiles, emit):
+    def apply(q_ref, rows, tiles, emit, begin, end):
         lane_at = lanes_of(rows)
-        for l in range(LV):
+        for l in range(begin, end):
             x = [q_ref[t, l, rows, :] for t in range(TILES)]
             to_low = [pltpu.roll(v, 127, 1) for v in x]
             to_high = [pltpu.roll(v, 1, 1) for v in x]
@@ -401,11 +460,21 @@
         for i, product in enumerate(products):
             sums[i] = sums[i] + fold(product)
 
-    apply(Q0, near, TILES, emit0)
-    clear_rows(Q1, TILES, 2)
-    apply(Q1, slice(LOW - 1, HIGH + 1), TILES, emit1)
-    clear_rows(Q2, TILES, 1)
-    apply(Q2, OWN_ROWS, 2, emit2)
+    def applications(begin, end):
+        step = 1 if begin else 0
+        apply(Q0, near, TILES, emit0, begin, end)
+        clear_rows(Q1, TILES, 0, 2, (begin, end - begin))
+        more = 0 if begin else 1
+        begin, end = begin + step, end + more
+        apply(Q1, slice(LOW - 1, HIGH + 1), TILES, emit1, begin, end)
+        clear_rows(Q2, TILES, 0, 1, (begin, end - begin))
+        begin, end = begin + step, end + more
+        apply(Q2, OWN_ROWS, 2, emit2, begin, end)
+
+    land_basis(deep_copies, deep, RL2, RH2)
+    applications(NS + 1, LV)
+    land_basis(coupled_copies, coupled, RL3, RH3)
+    applications(0, NS + 1)
 
     one_lane = lax.broadcasted_iota(jnp.int32, (1, 128), 1)
     packed = jnp.zeros((1, 128), F32)
@@ -497,14 +566,18 @@
             pack,
             landing,
             landing,
+            pack,
+            pack,
+            landing,
+            landing,
             pltpu.VMEM((8, 128), F32),
             pltpu.VMEM((64, 128), F32),
             pltpu.SemaphoreType.DMA((9,)),
-            pltpu.SemaphoreType.DMA((24,)),
-            pltpu.SemaphoreType.DMA((24,)),
+            pltpu.SemaphoreType.DMA((32,)),
+            pltpu.SemaphoreType.DMA((32,)),
         ],
         compiler_params=pltpu.CompilerParams(
-            collective_id=0, has_side_effects=True, vmem_limit_bytes=63 * 1024 * 1024
+            collective_id=0, has_side_effects=True, vmem_limit_bytes=66_000_000
         ),
     )(state, conduct, storage, surface, kinds, ptab.T, jnp.transpose(lw, (2, 0, 1)), rows, rw)
 

time: 49 us -> 43.6 us (0.89)
  Pallas kernels: 44.6 us -> 39.2 us
    pallas_call x1, Pallas kernels: 44.6 us -> 39.2 us  [body(): pl.pallas_call(kernel, out_shape=(jax.ShapeDtypeStruct((1, LV, RX, CY), F...]
where the time goes in v3:
time: 43.6 us; the launch traced here: 43.4 us
  Pallas kernels  39.2 us (90%)
  local copies, waits for them, and re-layouts  2.87 us (7%)
  between operations  1.29 us (3%)
    pallas_call x1, Pallas kernels, body(): pl.pallas_call(kernel, out_shape=(jax.ShapeDtypeStruct((1, LV, RX, CY), F...  39.2 us
    unnamed x4, local copies, waits for them, and re-layouts  2.87 us

profile of v3, /device:TPU:1, one launch (start us, length us, event | category | flops | bytes accessed | tf_op | source)
XLA Modules:
  0.0 43.4 jit_solution(18376926588761453004)
XLA Ops:
  1.3 39.2 %shard_map.104 = (f32[1,30,32,256]{3,2,1,0:T(8,128)}, f32[1,32,256]{2,1,0:T(8,128)}) custom-call(f32[1,30,32,256]{3,2,1,0:T(8,128)} %state.1, f32[1,30,32,256]{3,2,1,0:T(8,128)} %conduct.1, f32[1]{0:T(128)S(6)} %copy.13.storage, f32[1,32,256]{2,1,0:T(8,128)} %surface.1, s32[1,32,256]{2,1,0:T(8,128)} %kinds_in.1, f32[2,16]{1,0:T(2,128)} %bitcast.3, ...), custom_call_target="tpu_custom_call" | custom-call | tf_op jit(solution)/shard_map/pallas_call | solution.py:535
  40.5 0.0 copy-start
  40.5 2.3 %copy.14 = f32[1,30,32,256]{3,2,1,0:T(8,128)} copy(f32[1,30,32,256]{3,2,1,0:T(8,128)} %get-tuple-element.4) | data formatting | bytes 1966080
  42.8 0.0 copy-done
  42.8 0.6 %copy.15 = f32[1,32,256]{2,1,0:T(8,128)} copy(f32[1,32,256]{2,1,0:T(8,128)S(1)} %copy-done) | data formatting | bytes 65536
Async XLA Ops:
  40.5 2.3 %copy-start = (f32[1,32,256]{2,1,0:T(8,128)S(1)}, f32[1,32,256]{2,1,0:T(8,128)}, u32[]{:S(2)}) copy-start(f32[1,32,256]{2,1,0:T(8,128)} %get-tuple-element.5) | copy-start | bytes 98308

commit v4 on v3

--- a/solution.py
+++ b/solution.py
@@ -86,9 +86,13 @@
     RH3,
     ROW,
     GATH,
+    NEW,
+    FLUX,
     lsem,
     ssem,
     rsem,
+    near_sem,
+    far_sem,
 ):
     c, gx, gy = lax.axis_index("comp"), lax.axis_index("gx"), lax.axis_index("gy")
     xp, xm = lax.rem(gx + 1, 8), lax.rem(gx + 7, 8)
@@ -119,7 +123,13 @@
         for dx, dh, dz, co in far_first()
     ]
     barrier = pltpu.get_barrier_semaphore()
-    for peer in peers + [partner]:
+    ring = [(i, j) for i in (0, 1, -1) for j in (0, 1, -1) if (i, j) != (0, 0)]
+
+    def at_offset(i, j):
+        return (c, lax.rem(gx + 8 + i, 8), lax.rem(gy + 8 + j, 8))
+
+    neighbours = [at_offset(i, j) for i, j in ring]
+    for peer in neighbours + [partner]:
         pl.semaphore_signal(barrier, inc=1, device_id=peer, device_id_type=MESH)
 
     for copy in local[:4]:
@@ -146,7 +156,7 @@
     PL1[...] = low
     PH1[...] = high
 
-    pl.semaphore_wait(barrier, len(peers) + 1)
+    pl.semaphore_wait(barrier, len(neighbours) + 1)
 
     sends = []
 
@@ -200,6 +210,9 @@
     first = send_rows(S, 0, 1, every) + send_rows(K, 0, 1, every) + send_packs(PL1, PH1, RL1, RH1)
     levels_copy = send(state.at[0, pl.ds(0, NS)], PART, partner)
     rest = send_corners(PL1, PH1, RL1, RH1) + send_rows(K, 1, RIM - 1, every)
+
+    for peer in neighbours:
+        pl.semaphore_signal(near_sem, inc=1, device_id=peer, device_id_type=MESH)
 
     for copy in local[4:]:
         copy.wait()
@@ -344,6 +357,9 @@
         residual(l, NS)
     deep = (NS, LV - NS)
     deep_copies = send_basis(deep, PL2, PH2, RL2, RH2)
+    pl.semaphore_wait(near_sem, len(neighbours))
+    for i, j in ring:
+        pl.semaphore_signal(far_sem, inc=1, device_id=at_offset(2 * i, 2 * j), device_id_type=MESH)
     for l in range(NS):
         residual(l, 0)
 
@@ -373,7 +389,9 @@
     air = jnp.where(is_air, own, other)
     soil = jnp.where(is_air, other, own)
     flux = TAB[0] * (TAB[1] * soil - air)
-    flux_out[0] = flux
+    FLUX[...] = flux
+    results = [pltpu.make_async_copy(FLUX, flux_out.at[0], lsem.at[9])]
+    results[0].start()
     signed = jnp.where(is_air, flux, -flux)
     for l in range(NS):
         top = signed * TAB[2 + l]
@@ -418,7 +436,7 @@
         clear_rows(Q0, 2, 0, RIM, levels)
         fill_rim(Q0, from_low, from_high, wide, levels)
 
-    shift = storage[0]
+    shift = storage[0, 0]
     scale = 1.0 / SHIFT
 
     def apply(q_ref, rows, tiles, emit, begin, end):
@@ -483,6 +501,7 @@
     me = gx * 8 + gy
     ROW[0:1, :] = packed
     GATH[pl.ds(me, 1), :] = packed
+    pl.semaphore_wait(far_sem, len(ring))
     for peer in peers:
         pltpu.make_async_remote_copy(
             src_ref=ROW.at[pl.ds(0, 1)],
@@ -512,34 +531,57 @@
 
     for l in range(LV):
         for t in range(2):
-            out[0, l, :, 128 * t : 128 * t + 128] = (
+            NEW[l, :, 128 * t : 128 * t + 128] = (
                 S[t, l, OWN_ROWS, :]
                 + y0 * Q0[t, l, OWN_ROWS, :]
                 + y1 * Q1[t, l, OWN_ROWS, :]
                 + y2 * Q2[t, l, OWN_ROWS, :]
             )
+        if l % 6 == 5:
+            done = pl.ds(l - 5, 6)
+            results.append(
+                pltpu.make_async_copy(NEW.at[done], out.at[0, done], lsem.at[9 + len(results)])
+            )
+            results[-1].start()
     pltpu.make_async_copy(all_rows, all_rows, lsem.at[7]).wait()
     for copy in sends:
         copy.wait_send()
+    for copy in results:
+        copy.wait()
+
+
+def deliver(fields, flux, fields_out, flux_out, held, held_flux, sem_in, sem_out):
+    thirds = [pl.ds(i * (LV // 3), LV // 3) for i in range(3)]
+    copies = [(fields.at[0, at], held.at[at], fields_out.at[0, at]) for at in thirds]
+    copies.append((flux, held_flux, flux_out))
+    into = [pltpu.make_async_copy(a, b, sem_in.at[i]) for i, (a, b, _) in enumerate(copies)]
+    back = [pltpu.make_async_copy(b, c, sem_out.at[i]) for i, (_, b, c) in enumerate(copies)]
+    for copy in into:
+        copy.start()
+    for arrived, copy in zip(into, back):
+        arrived.wait()
+        copy.start()
+    for copy in back:
+        copy.wait()
 
 
 def body(state, conduct, storage, surface, kinds, ptab, lw, rows, rw):
     hbm = pl.BlockSpec(memory_space=pltpu.HBM)
     smem = pl.BlockSpec(memory_space=pltpu.SMEM)
-    vmem = pl.BlockSpec(memory_space=pltpu.VMEM)
     field = pltpu.VMEM((TILES, LV, EX, 128), F32)
     inner = pltpu.VMEM((2, LV, EX, 128), F32)
     plane = pltpu.VMEM((RX, CY), F32)
     pack = pltpu.VMEM((RX, 128), F32)
     landing = pltpu.VMEM((EX, 128), F32)
-    return pl.pallas_call(
+    shapes = (
+        jax.ShapeDtypeStruct((1, LV, RX, CY), F32),
+        jax.ShapeDtypeStruct((1, RX, CY), F32),
+    )
+    fields, flux = pl.pallas_call(
         kernel,
-        out_shape=(
-            jax.ShapeDtypeStruct((1, LV, RX, CY), F32),
-            jax.ShapeDtypeStruct((1, RX, CY), F32),
-        ),
+        out_shape=shapes,
         in_specs=[hbm, hbm, smem, hbm, hbm, smem, smem, smem, hbm],
-        out_specs=(vmem, vmem),
+        out_specs=(hbm, hbm),
         scratch_shapes=[
             inner,
             field,
@@ -572,14 +614,31 @@
             landing,
             pltpu.VMEM((8, 128), F32),
             pltpu.VMEM((64, 128), F32),
-            pltpu.SemaphoreType.DMA((9,)),
+            pltpu.VMEM((LV, RX, CY), F32),
+            plane,
+            pltpu.SemaphoreType.DMA((16,)),
             pltpu.SemaphoreType.DMA((32,)),
             pltpu.SemaphoreType.DMA((32,)),
+            pltpu.SemaphoreType.REGULAR,
+            pltpu.SemaphoreType.REGULAR,
         ],
         compiler_params=pltpu.CompilerParams(
             collective_id=0, has_side_effects=True, vmem_limit_bytes=66_000_000
         ),
-    )(state, conduct, storage, surface, kinds, ptab.T, jnp.transpose(lw, (2, 0, 1)), rows, rw)
+    )(state, conduct, storage.reshape(1, 1), surface, kinds, ptab.T, jnp.transpose(lw, (2, 0, 1)), rows, rw)
+    return pl.pallas_call(
+        deliver,
+        out_shape=shapes,
+        in_specs=[hbm, hbm],
+        out_specs=(hbm, hbm),
+        scratch_shapes=[
+            pltpu.VMEM((LV, RX, CY), F32),
+            pltpu.VMEM((1, RX, CY), F32),
+            pltpu.SemaphoreType.DMA((4,)),
+            pltpu.SemaphoreType.DMA((4,)),
+        ],
+        compiler_params=pltpu.CompilerParams(vmem_limit_bytes=66_000_000),
+    )(fields, flux)
 
 
 def solution(mesh):

time: 43.6 us -> 41.2 us (0.945)
  local copies, waits for them, and re-layouts: 2.87 us -> 0 us
  Pallas kernels: 39.2 us -> 39.7 us
    unnamed x4 -> x0, local copies, waits for them, and re-layouts: 2.87 us -> none
    pallas_call x1 -> x2, Pallas kernels: 39.2 us -> 39.7 us  [the longest x1 37.8 us: body(): pl.pallas_call(kernel, out_shape=shapes, in_specs=[hbm, hbm, smem, hbm, h...]
where the time goes in v4:
time: 41.2 us; the launch traced here: 41 us
  Pallas kernels  39.7 us (96%)
  between operations  1.29 us (3%)
    pallas_call x1, Pallas kernels, body(): pl.pallas_call(kernel, out_shape=shapes, in_specs=[hbm, hbm, smem, hbm, h...  37.8 us
    pallas_call x1, Pallas kernels, body(): pl.pallas_call(deliver, out_shape=shapes, in_specs=[hbm, hbm], out_specs=...  1.98 us

profile of v4, /device:TPU:1, one launch (start us, length us, event | category | flops | bytes accessed | tf_op | source)
XLA Modules:
  0.0 41.0 jit_solution(12522937861089233548)
XLA Ops:
  1.3 37.8 %shard_map.104 = (f32[1,30,32,256]{3,2,1,0:T(8,128)}, f32[1,32,256]{2,1,0:T(8,128)}) custom-call(f32[1,30,32,256]{3,2,1,0:T(8,128)} %state.1, f32[1,30,32,256]{3,2,1,0:T(8,128)} %conduct.1, f32[1,1]{1,0:T(1,128)} %bitcast.3.storage, f32[1,32,256]{2,1,0:T(8,128)} %surface.1, s32[1,32,256]{2,1,0:T(8,128)} %kinds_in.1, f32[2,16]{1,0:T(2,128)} %bitcast.5, ...), custom_call_target="tpu_custom_call" | custom-call | tf_op jit(solution)/shard_map/pallas_call | solution.py:580
  39.0 2.0 %shard_map.105 = (f32[1,30,32,256]{3,2,1,0:T(8,128)}, f32[1,32,256]{2,1,0:T(8,128)}) custom-call(f32[1,30,32,256]{3,2,1,0:T(8,128)} %get-tuple-element.4.fields, f32[1,32,256]{2,1,0:T(8,128)} %get-tuple-element.5.flux), custom_call_target="tpu_custom_call" | custom-call | tf_op jit(solution)/shard_map/pallas_call | solution.py:629

commit v5 on v4

--- a/solution.py
+++ b/solution.py
@@ -18,6 +18,7 @@
 EX = 48
 LOW, HIGH = 8, 40
 OWN_ROWS = slice(LOW, HIGH)
+INNER = slice(LOW + 4, HIGH - 4)
 EDGE = 96
 SHIFT = 7.0
 HP = lax.Precision.HIGHEST
@@ -25,10 +26,6 @@
 
 def shifted(rows, by):
     return slice(rows.start + by, rows.stop + by)
-
-
-def fold(x):
-    return (x[0:8] + x[8:16]) + (x[16:24] + x[24:32])
 
 
 def far_first():
@@ -123,12 +120,10 @@
         for dx, dh, dz, co in far_first()
     ]
     barrier = pltpu.get_barrier_semaphore()
-    ring = [(i, j) for i in (0, 1, -1) for j in (0, 1, -1) if (i, j) != (0, 0)]
-
     def at_offset(i, j):
         return (c, lax.rem(gx + 8 + i, 8), lax.rem(gy + 8 + j, 8))
 
-    neighbours = [at_offset(i, j) for i, j in ring]
+    neighbours = [at_offset(i, j) for i, j in ((1, 0), (-1, 0), (0, 1), (0, -1))]
     for peer in neighbours + [partner]:
         pl.semaphore_signal(barrier, inc=1, device_id=peer, device_id_type=MESH)
 
@@ -209,10 +204,7 @@
     every = (0, LV)
     first = send_rows(S, 0, 1, every) + send_rows(K, 0, 1, every) + send_packs(PL1, PH1, RL1, RH1)
     levels_copy = send(state.at[0, pl.ds(0, NS)], PART, partner)
-    rest = send_corners(PL1, PH1, RL1, RH1) + send_rows(K, 1, RIM - 1, every)
-
-    for peer in neighbours:
-        pl.semaphore_signal(near_sem, inc=1, device_id=peer, device_id_type=MESH)
+    rest = send_rows(K, 1, RIM - 1, every)
 
     for copy in local[4:]:
         copy.wait()
@@ -247,6 +239,12 @@
     for copy in first:
         copy.wait_recv()
 
+    near_ring = [(i, j) for i in range(-2, 3) for j in range(-2, 3) if abs(i) + abs(j) == 2]
+    far_ring = [(4, 0), (0, 4), (2, 2), (2, -2), (-2, 2), (-2, -2)]
+    rest += send_corners(PL1, PH1, RL1, RH1)
+    for i, j in near_ring:
+        pl.semaphore_signal(near_sem, inc=1, device_id=at_offset(i, j), device_id_type=MESH)
+
     row = lax.broadcasted_iota(jnp.int32, (EX, 128), 0)
     row_ok = (
         ((row >= LOW) & (row < HIGH))
@@ -357,9 +355,6 @@
         residual(l, NS)
     deep = (NS, LV - NS)
     deep_copies = send_basis(deep, PL2, PH2, RL2, RH2)
-    pl.semaphore_wait(near_sem, len(neighbours))
-    for i, j in ring:
-        pl.semaphore_signal(far_sem, inc=1, device_id=at_offset(2 * i, 2 * j), device_id_type=MESH)
     for l in range(NS):
         residual(l, 0)
 
@@ -402,39 +397,64 @@
 
     coupled = (0, NS)
     coupled_copies = send_basis(coupled, PL3, PH3, RL3, RH3)
-
-    for copy in rest:
-        copy.wait_recv()
-    clean_packs(RL1, RH1, (slice(0, LOW), slice(HIGH, EX)))
-    clear_rows(K, 2, 1, RIM - 1, every)
-    fill_rim(K, RL1, RH1, wide, every)
-    for l in range(LV + 1):
-        for rows in (slice(LOW - 2, LOW), slice(HIGH, HIGH + 2)):
+    pl.semaphore_wait(near_sem, len(near_ring))
+    for i, j in far_ring:
+        pl.semaphore_signal(far_sem, inc=1, device_id=at_offset(i, j), device_id_type=MESH)
+
+    low_rim, high_rim = slice(LOW - RIM, LOW), slice(HIGH, HIGH + RIM)
+
+    def beside_pairs(l, rows, tiles):
+        lane_at = lanes_of(rows)
+        k = [K[t, l, rows, :] for t in range(TILES)]
+        for t in tiles:
+            beyond, before = pltpu.roll(k[(t + 1) % 3], 127, 1), pltpu.roll(k[(t + 2) % 3], 1, 1)
+            right = jnp.where(lane_at == 127, beyond, pltpu.roll(k[t], 127, 1))
+            left = jnp.where(lane_at == 0, before, pltpu.roll(k[t], 1, 1))
+            KY[t, l, rows, :] = 0.5 * (k[t] + right)
+            KYM[t, l, rows, :] = 0.5 * (k[t] + left)
+
+    def pairs_right_left():
+        fill_rim(K, RL1, RH1, OWN_ROWS, every)
+        for l in range(LV + 1):
+            vertical(2, l, OWN_ROWS)
+            if l < LV:
+                along_rows(2, l, slice(LOW, HIGH - 1))
+                beside_pairs(l, OWN_ROWS, (2,))
+
+    def pairs_above_below():
+        for copy in rest:
+            copy.wait_recv()
+        clean_packs(RL1, RH1, (slice(0, LOW), slice(HIGH, EX)))
+        clear_rows(K, 2, 1, RIM - 1, every)
+        fill_rim(K, RL1, RH1, low_rim, every)
+        fill_rim(K, RL1, RH1, high_rim, every)
+        for l in range(LV + 1):
+            for rows in (slice(LOW - 2, LOW), slice(HIGH, HIGH + 2)):
+                for t in range(TILES):
+                    vertical(t, l, rows)
+                if l < LV:
+                    beside_pairs(l, rows, range(TILES))
+            if l == LV:
+                break
             for t in range(2):
-                vertical(t, l, rows)
-        vertical(2, l, near)
-        if l == LV:
-            break
-        for t in range(2):
-            along_rows(t, l, slice(LOW - 3, LOW - 1))
-            along_rows(t, l, slice(HIGH, HIGH + 2))
-        along_rows(2, l, slice(LOW - 3, HIGH + 2))
-        for rows, tiles in ((slice(LOW - 2, LOW), (0, 1)), (slice(HIGH, HIGH + 2), (0, 1)), (near, (2,))):
-            lane_at = lanes_of(rows)
-            k = [K[t, l, rows, :] for t in range(TILES)]
-            for t in tiles:
-                beyond, before = pltpu.roll(k[(t + 1) % 3], 127, 1), pltpu.roll(k[(t + 2) % 3], 1, 1)
-                right = jnp.where(lane_at == 127, beyond, pltpu.roll(k[t], 127, 1))
-                left = jnp.where(lane_at == 0, before, pltpu.roll(k[t], 1, 1))
-                KY[t, l, rows, :] = 0.5 * (k[t] + right)
-                KYM[t, l, rows, :] = 0.5 * (k[t] + left)
-
-    def land_basis(copies, levels, from_low, from_high):
+                along_rows(t, l, slice(LOW - 3, LOW - 1))
+                along_rows(t, l, slice(HIGH, HIGH + 2))
+            along_rows(2, l, slice(LOW - 3, LOW))
+            along_rows(2, l, slice(HIGH - 1, HIGH + 2))
+
+    def land_columns(copies, levels, from_low, from_high):
         for copy in copies:
             copy.wait_recv()
-        clean_packs(from_low, from_high, (slice(0, EX),))
+        clean_packs(from_low, from_high, (OWN_ROWS,))
+        fill_rim(Q0, from_low, from_high, OWN_ROWS, levels)
+
+    def land_rows(copies, levels, from_low, from_high):
+        for copy in copies:
+            copy.wait_recv()
+        clean_packs(from_low, from_high, (slice(0, LOW), slice(HIGH, EX)))
         clear_rows(Q0, 2, 0, RIM, levels)
-        fill_rim(Q0, from_low, from_high, wide, levels)
+        fill_rim(Q0, from_low, from_high, low_rim, levels)
+        fill_rim(Q0, from_low, from_high, high_rim, levels)
 
     shift = storage[0, 0]
     scale = 1.0 / SHIFT
@@ -458,7 +478,7 @@
         if t < 2:
             W0[t, l, rows, :] = shift * x + total
         else:
-            q = q * rim_mask
+            q = q * rim_mask[0 : rows.stop - rows.start]
         Q1[t, l, rows, :] = q
 
     def emit1(l, t, x, total, rows):
@@ -470,29 +490,52 @@
         Q2[t, l, rows, :] = q
 
     sums = [jnp.zeros((8, 128), F32) for _ in range(9)]
+    edge_sums = [jnp.zeros((4, 128), F32) for _ in range(9)]
 
     def emit2(l, t, x, total, rows):
         w2 = shift * x + total
         w0, w1, q0 = W0[t, l, rows, :], W1[t, l, rows, :], Q0[t, l, rows, :]
         products = (w0 * q0, w0 * w0, w1 * q0, w1 * w0, w1 * w1, w2 * q0, w2 * w0, w2 * w1, w2 * w2)
         for i, product in enumerate(products):
-            sums[i] = sums[i] + fold(product)
-
-    def applications(begin, end):
-        step = 1 if begin else 0
-        apply(Q0, near, TILES, emit0, begin, end)
-        clear_rows(Q1, TILES, 0, 2, (begin, end - begin))
-        more = 0 if begin else 1
+            if rows == INNER:
+                sums[i] = sums[i] + ((product[0:8] + product[8:16]) + product[16:24])
+            else:
+                edge_sums[i] = edge_sums[i] + product
+
+    def applications(begin, end, inside):
+        step, more = (1, 0) if begin else (0, 1)
+        if inside:
+            passes = ((slice(9, 39),), (slice(10, 38),), (INNER,))
+        else:
+            passes = (
+                (slice(6, 9), slice(39, 42)),
+                (slice(7, 10), slice(38, 41)),
+                (slice(8, 12), slice(36, 40)),
+            )
+        for rows in passes[0]:
+            apply(Q0, rows, TILES, emit0, begin, end)
+        if not inside:
+            clear_rows(Q1, TILES, 0, 2, (begin, end - begin))
         begin, end = begin + step, end + more
-        apply(Q1, slice(LOW - 1, HIGH + 1), TILES, emit1, begin, end)
-        clear_rows(Q2, TILES, 0, 1, (begin, end - begin))
+        for rows in passes[1]:
+            apply(Q1, rows, TILES, emit1, begin, end)
+        if not inside:
+            clear_rows(Q2, TILES, 0, 1, (begin, end - begin))
         begin, end = begin + step, end + more
-        apply(Q2, OWN_ROWS, 2, emit2, begin, end)
-
-    land_basis(deep_copies, deep, RL2, RH2)
-    applications(NS + 1, LV)
-    land_basis(coupled_copies, coupled, RL3, RH3)
-    applications(0, NS + 1)
+        for rows in passes[2]:
+            apply(Q2, rows, 2, emit2, begin, end)
+
+    pairs_right_left()
+    land_columns(deep_copies[-2:], deep, RL2, RH2)
+    applications(NS + 1, LV, True)
+    land_columns(coupled_copies[-2:], coupled, RL3, RH3)
+    applications(0, NS + 1, True)
+    pairs_above_below()
+    land_rows(deep_copies[:-2], deep, RL2, RH2)
+    applications(NS + 1, LV, False)
+    land_rows(coupled_copies[:-2], coupled, RL3, RH3)
+    applications(0, NS + 1, False)
+    sums = [(a[0:4] + a[4:8]) + b for a, b in zip(sums, edge_sums)]
 
     one_lane = lax.broadcasted_iota(jnp.int32, (1, 128), 1)
     packed = jnp.zeros((1, 128), F32)
@@ -501,7 +544,7 @@
     me = gx * 8 + gy
     ROW[0:1, :] = packed
     GATH[pl.ds(me, 1), :] = packed
-    pl.semaphore_wait(far_sem, len(ring))
+    pl.semaphore_wait(far_sem, len(far_ring))
     for peer in peers:
         pltpu.make_async_remote_copy(
             src_ref=ROW.at[pl.ds(0, 1)],

time: 41.2 us -> 39.7 us (0.964)
  Pallas kernels: 39.7 us -> 38.2 us
    pallas_call x1, Pallas kernels: 37.8 us -> 36.2 us  [body(): pl.pallas_call(kernel, out_shape=shapes, in_specs=[hbm, hbm, smem, hbm, h...]
where the time goes in v5:
time: 39.7 us; the launch traced here: 39.5 us
  Pallas kernels  38.2 us (96%)
  between operations  1.29 us (3%)
    pallas_call x1, Pallas kernels, body(): pl.pallas_call(kernel, out_shape=shapes, in_specs=[hbm, hbm, smem, hbm, h...  36.2 us
    pallas_call x1, Pallas kernels, body(): pl.pallas_call(deliver, out_shape=shapes, in_specs=[hbm, hbm], out_specs=...  1.98 us

profile of v5, /device:TPU:1, one launch (start us, length us, event | category | flops | bytes accessed | tf_op | source)
XLA Modules:
  0.0 39.5 jit_solution(2069329246588412404)
XLA Ops:
  1.3 36.2 %shard_map.104 = (f32[1,30,32,256]{3,2,1,0:T(8,128)}, f32[1,32,256]{2,1,0:T(8,128)}) custom-call(f32[1,30,32,256]{3,2,1,0:T(8,128)} %state.1, f32[1,30,32,256]{3,2,1,0:T(8,128)} %conduct.1, f32[1,1]{1,0:T(1,128)} %bitcast.3.storage, f32[1,32,256]{2,1,0:T(8,128)} %surface.1, s32[1,32,256]{2,1,0:T(8,128)} %kinds_in.1, f32[2,16]{1,0:T(2,128)} %bitcast.5, ...), custom_call_target="tpu_custom_call" | custom-call | tf_op jit(solution)/shard_map/pallas_call | solution.py:623
  37.5 2.0 %shard_map.105 = (f32[1,30,32,256]{3,2,1,0:T(8,128)}, f32[1,32,256]{2,1,0:T(8,128)}) custom-call(f32[1,30,32,256]{3,2,1,0:T(8,128)} %get-tuple-element.4.fields, f32[1,32,256]{2,1,0:T(8,128)} %get-tuple-element.5.flux), custom_call_target="tpu_custom_call" | custom-call | tf_op jit(solution)/shard_map/pallas_call | solution.py:672

commit v6 on v5

--- a/solution.py
+++ b/solution.py
@@ -203,7 +203,8 @@
 
     every = (0, LV)
     first = send_rows(S, 0, 1, every) + send_rows(K, 0, 1, every) + send_packs(PL1, PH1, RL1, RH1)
-    levels_copy = send(state.at[0, pl.ds(0, NS)], PART, partner)
+    halves = [pl.ds(0, NS // 2), pl.ds(NS // 2, NS // 2)]
+    levels_copies = [send(state.at[0, half], PART.at[half], partner) for half in halves]
     rest = send_rows(K, 1, RIM - 1, every)
 
     for copy in local[4:]:
@@ -343,13 +344,14 @@
             Q0[t, l, OWN_ROWS, :] = -flow(S, l, t, s[t], OWN_ROWS, right, left)
 
     def send_basis(levels, pack_low, pack_high, from_low, from_high):
+        made = send_rows(Q0, 0, RIM, levels)
         low, high = blank, blank
         for l in range(levels[0], levels[0] + levels[1]):
             low, high = edges(Q0[0, l, OWN_ROWS, :], Q0[1, l, OWN_ROWS, :], l, low, high)
         pack_low[...] = low
         pack_high[...] = high
         packs = (pack_low, pack_high, from_low, from_high)
-        return send_corners(*packs) + send_rows(Q0, 0, RIM, levels) + send_packs(*packs)
+        return made + send_corners(*packs) + send_packs(*packs)
 
     for l in range(NS, LV):
         residual(l, NS)
@@ -358,27 +360,29 @@
     for l in range(NS):
         residual(l, 0)
 
-    levels_copy.wait_recv()
-    received = PART[...].reshape(NS * RX, CY)
-    mixed = jnp.concatenate(
-        [
-            lax.dot_general(
-                received[:, b : b + PATCH],
-                RW[b : b + PATCH, :],
-                (((1,), (1,)), ((), ())),
-                precision=HP,
-                preferred_element_type=F32,
+    other = jnp.zeros((RX, CY), F32)
+    for h, copy in enumerate(levels_copies):
+        copy.wait_recv()
+        begin = h * (NS // 2)
+        received = PART[begin : begin + NS // 2].reshape(NS // 2 * RX, CY)
+        mixed = jnp.concatenate(
+            [
+                lax.dot_general(
+                    received[:, b : b + PATCH],
+                    RW[b : b + PATCH, :],
+                    (((1,), (1,)), ((), ())),
+                    precision=HP,
+                    preferred_element_type=F32,
+                )
+                for b in range(0, CY, PATCH)
+            ],
+            axis=1,
+        )
+        for l in range(NS // 2):
+            remapped = jnp.dot(
+                picker, mixed[l * RX : (l + 1) * RX], precision=HP, preferred_element_type=F32
             )
-            for b in range(0, CY, PATCH)
-        ],
-        axis=1,
-    )
-    other = jnp.zeros((RX, CY), F32)
-    for l in range(NS):
-        remapped = jnp.dot(
-            picker, mixed[l * RX : (l + 1) * RX], precision=HP, preferred_element_type=F32
-        )
-        other = other + TAB[2 + NS + l] * remapped
+            other = other + TAB[2 + NS + begin + l] * remapped
     own = OWN[...]
     is_air = c == 0
     air = jnp.where(is_air, own, other)

time: 39.7 us -> 39.6 us (level)
  no operation moved by 1% of the time
where the time goes in v6:
time: 39.6 us; the launch traced here: 39.4 us
  Pallas kernels  38.1 us (96%)
  between operations  1.29 us (3%)
    pallas_call x1, Pallas kernels, body(): pl.pallas_call(kernel, out_shape=shapes, in_specs=[hbm, hbm, smem, hbm, h...  36.1 us
    pallas_call x1, Pallas kernels, body(): pl.pallas_call(deliver, out_shape=shapes, in_specs=[hbm, hbm], out_specs=...  1.98 us

profile of v6, /device:TPU:1, one launch (start us, length us, event | category | flops | bytes accessed | tf_op | source)
XLA Modules:
  0.0 39.4 jit_solution(14731289037819518329)
XLA Ops:
  1.3 36.1 %shard_map.104 = (f32[1,30,32,256]{3,2,1,0:T(8,128)}, f32[1,32,256]{2,1,0:T(8,128)}) custom-call(f32[1,30,32,256]{3,2,1,0:T(8,128)} %state.1, f32[1,30,32,256]{3,2,1,0:T(8,128)} %conduct.1, f32[1,1]{1,0:T(1,128)} %bitcast.3.storage, f32[1,32,256]{2,1,0:T(8,128)} %surface.1, s32[1,32,256]{2,1,0:T(8,128)} %kinds_in.1, f32[2,16]{1,0:T(2,128)} %bitcast.5, ...), custom_call_target="tpu_custom_call" | custom-call | tf_op jit(solution)/shard_map/pallas_call | solution.py:627
  37.4 2.0 %shard_map.105 = (f32[1,30,32,256]{3,2,1,0:T(8,128)}, f32[1,32,256]{2,1,0:T(8,128)}) custom-call(f32[1,30,32,256]{3,2,1,0:T(8,128)} %get-tuple-element.4.fields, f32[1,32,256]{2,1,0:T(8,128)} %get-tuple-element.5.flux), custom_call_target="tpu_custom_call" | custom-call | tf_op jit(solution)/shard_map/pallas_call | solution.py:676
